TPU v7x, 512 devices: a whole 4x8x8 slice. The times are simulated.
512 devices in a mesh: xt: 32 (over z, x), yt: 16 (over y, core).
Axes of the slice: x: 4, y: 8, z: 8, core: 2. Of those that a mesh axis runs over, the one named last changes fastest.
Arguments:
- pressure: float32 [8, 256, 2048], P(None, 'xt', 'yt'), may hold values from -1 to 1
- saturation: float32 [2, 8, 256, 2048], P(None, None, 'xt', 'yt'), may hold values from 0.05 to 0.45
- old_mass: float32 [3, 8, 256, 2048], P(None, None, 'xt', 'yt'), may hold values from 0.05 to 0.5
- pore_volume: float32 [8, 256, 2048], P(None, 'xt', 'yt'), may hold values from 0.2 to 2
- transmissibility: float32 [3, 8, 256, 2048], P(None, None, 'xt', 'yt'), may hold values from 1 to 10
- upwind_code: int32 [8, 256, 2048], P(None, 'xt', 'yt'), may hold values from 0 to 511
- cell_tangent: float32 [2, 3, 8, 256, 2048], P(None, None, None, 'xt', 'yt'), may hold values from -6 to 6
- segment_pressure: float32 [128, 4096], P('yt', 'xt'), may hold values from -1 to 1
- segment_tangent: float32 [2, 128, 4096], P(None, 'yt', 'xt'), may hold values from -6 to 6
- segment_well: int32 [128, 4096], P('yt', 'xt'), may hold values from 0 to 255, never falling along the last dimension, each value on 1 to 32 neighbouring positions
- link_factor: float32 [128, 4096], P('yt', 'xt'), may hold values from 0.5 to 5
- heel_pressure: float32 [128, 4096], P('yt', 'xt'), may hold values from -2 to 0
- perforation_cell: int32 [16, 16384], P('yt', 'xt'), may hold values from 0 to 8191
- perforation_segment: int32 [16, 16384], P('yt', 'xt'), may hold values from 0 to 1023
- well_index: float32 [16, 16384], P('yt', 'xt'), may hold values from 1 to 10
- perforation_count: int32 [16, 1024], P('yt', 'xt'), may hold values from 0 to 16, as said below
Outputs:
- residual: float32 [3, 8, 256, 2048], P(None, None, 'xt', 'yt')
- cell_products: float32 [2, 3, 8, 256, 2048], P(None, None, None, 'xt', 'yt')
- segment_residual: float32 [3, 128, 4096], P(None, 'yt', 'xt')
Inputs may be any that keep to these rules, and one draw needn't show every extreme that they name: `upwind_code`: bit 3 * d + a set: phase a on the face after the cell along direction d takes the mobility of the next cell. `perforation_cell`: local number of a cell of the slot's own device. `perforation_segment`: slot k * 16 + m names a segment of the device with xt index k and the same yt index, by its number r * 128 + c in that device's block. `perforation_count`: entry k of a device: how many of its slots toward xt index k are live (the first ones). For each yt index some xt index gets 16 from every device of that yt index. `segment_well`: never falls along a row; a run of equal numbers is one well.
All inputs are finite; a program needn't handle non-finite values.
Results may differ from a plain program's by a relative error of at most 0.0003.
Values sent between devices are 32-bit elements; how exact they have to be, the bound alone decides.
No kernel may reach another device: no remote copies, remote signals or barrier semaphores. Data moves between devices by JAX's collectives and lax.ppermute only.
A program may use at most 128 MiB of HBM per device.

v0:
```python
import jax
import jax.numpy as jnp
from jax import lax
from jax.sharding import PartitionSpec as P

COMPRESS = (0.05, 0.1, 0.6)
VISCOSITY = (0.5, 2.0, 0.2)
GRAVITY_HEAD = (0.3, 0.25, 0.05)


def from_behind(array, axis, by):
    length = lax.axis_size(axis)
    pairs = [(i, i + by) for i in range(length) if 0 <= i + by < length]
    return lax.ppermute(array, axis, pairs)


def dual_product(left_term, right_term):
    return jnp.stack(
        [
            left_term[0] * right_term[0],
            left_term[1] * right_term[0] + left_term[0] * right_term[1],
            left_term[2] * right_term[0] + left_term[0] * right_term[2],
        ]
    )


def stream_properties(press_streams, water_streams, gas_streams):
    oil_streams = jnp.stack(
        [
            1.0 - water_streams[0] - gas_streams[0],
            -water_streams[1] - gas_streams[1],
            -water_streams[2] - gas_streams[2],
        ]
    )
    mobility_list = []
    mass_list = []
    for phase, phase_saturation in enumerate((water_streams, oil_streams, gas_streams)):
        density_base = jnp.exp(COMPRESS[phase] * press_streams[0])
        density = jnp.stack(
            [
                density_base,
                COMPRESS[phase] * density_base * press_streams[1],
                COMPRESS[phase] * density_base * press_streams[2],
            ]
        )
        phase_mass = dual_product(density, phase_saturation)
        mobility_list.append(dual_product(phase_mass, phase_saturation) / VISCOSITY[phase])
        mass_list.append(phase_mass)
    return (jnp.stack(mobility_list, 1), jnp.stack(mass_list, 1))


def phase_bits(code_array, direction):
    return jnp.stack([code_array // 2 ** (3 * direction + phase) % 2 for phase in range(3)])


def face_flux(
    mob_lower, mob_upper, press_lower, press_upper, trans_face, upwind_bits, gravity_head
):
    upwind_mob = jnp.where(upwind_bits[None] == 1, mob_upper, mob_lower)
    pressure_drop = (press_lower - press_upper)[:, None] + gravity_head
    return trans_face * dual_product(upwind_mob, pressure_drop)


def rim_values(received_press, received_other):
    return (received_press, received_other)


def rim_other(mob_streams, dim_at, start, stop):
    return lax.slice_in_dim(mob_streams, start, stop, axis=dim_at + 1)


def body(
    pressure,
    saturation,
    old_mass,
    pore_volume,
    transmissibility,
    upwind_code,
    cell_tangent,
    segment_pressure,
    segment_tangent,
    segment_well,
    link_factor,
    heel_pressure,
    perforation_cell,
    perforation_segment,
    well_index,
    perforation_count,
):
    layers, width_x, width_y = pressure.shape
    rows_seg, cols_seg = segment_pressure.shape
    tiles_x = lax.axis_size("xt")
    top_x = lax.axis_index("xt") == tiles_x - 1
    top_y = lax.axis_index("yt") == lax.axis_size("yt") - 1
    press_streams = jnp.concatenate([pressure[None], cell_tangent[:, 0]], 0)
    water_streams = jnp.concatenate([saturation[0][None], cell_tangent[:, 1]], 0)
    gas_streams = jnp.concatenate([saturation[1][None], cell_tangent[:, 2]], 0)
    mob_streams, mass_streams = stream_properties(press_streams, water_streams, gas_streams)
    balance_all = jnp.concatenate(
        [(pore_volume * mass_streams[0] - old_mass)[None], pore_volume * mass_streams[1:]], 0
    )
    seg_streams = jnp.concatenate([segment_pressure[None], segment_tangent], 0)
    well_float = segment_well.astype(jnp.float32)
    east_other = rim_other(mob_streams, 2, 0, 1)
    north_other = rim_other(mob_streams, 3, 0, 1)
    got_east = from_behind(
        (press_streams[:, :, 0:1, :], east_other, seg_streams[:, :, 0:1], well_float[:, 0:1]),
        "xt",
        -1,
    )
    got_north = from_behind((press_streams[:, :, :, 0:1], north_other), "yt", -1)
    east_press, east_mob = rim_values(got_east[0], got_east[1])
    north_press, north_mob = rim_values(got_north[0], got_north[1])
    flux_east = face_flux(
        mob_streams,
        jnp.concatenate([mob_streams[:, :, :, 1:, :], east_mob], 3),
        press_streams,
        jnp.concatenate([press_streams[:, :, 1:, :], east_press], 2),
        transmissibility[0],
        phase_bits(upwind_code, 0),
        0.0,
    )
    column_x = lax.broadcasted_iota(jnp.int32, (1, 1, 1, width_x, 1), 3)
    flux_east = jnp.where(jnp.logical_and(top_x, column_x == width_x - 1), 0.0, flux_east)
    flux_north = face_flux(
        mob_streams,
        jnp.concatenate([mob_streams[:, :, :, :, 1:], north_mob], 4),
        press_streams,
        jnp.concatenate([press_streams[:, :, :, 1:], north_press], 3),
        transmissibility[1],
        phase_bits(upwind_code, 1),
        0.0,
    )
    column_y = lax.broadcasted_iota(jnp.int32, (1, 1, 1, 1, width_y), 4)
    flux_north = jnp.where(jnp.logical_and(top_y, column_y == width_y - 1), 0.0, flux_north)
    gravity_head = (
        jnp.zeros((3, 3, 1, 1, 1), jnp.float32)
        .at[0, :, 0, 0, 0]
        .set(jnp.asarray(GRAVITY_HEAD, dtype=jnp.float32))
    )
    flux_down = face_flux(
        mob_streams[:, :, :-1],
        mob_streams[:, :, 1:],
        press_streams[:, :-1],
        press_streams[:, 1:],
        transmissibility[2][:-1],
        phase_bits(upwind_code[:-1], 2),
        gravity_head,
    )
    column_seg = lax.broadcasted_iota(jnp.int32, (rows_seg, cols_seg), 1)
    next_press = jnp.concatenate([seg_streams[:, :, 1:], got_east[2]], 2)
    next_well = jnp.concatenate([well_float[:, 1:], got_east[3]], 1)
    linked = jnp.logical_and(
        next_well == well_float, jnp.logical_not(jnp.logical_and(top_x, column_seg == cols_seg - 1))
    )
    heel_streams = jnp.stack(
        [heel_pressure, jnp.zeros_like(heel_pressure), jnp.zeros_like(heel_pressure)]
    )
    link_flow = link_factor * (seg_streams - jnp.where(linked, next_press, heel_streams))
    carried = jnp.where(linked, link_flow, 0.0)
    got_back = from_behind((flux_east[:, :, :, -1:, :], carried[:, :, -1:]), "xt", 1)
    flux_south = from_behind(flux_north[:, :, :, :, -1:], "yt", 1)
    flux_west = got_back[0]
    carried_in = got_back[1]
    balance_all = (
        balance_all
        + flux_east
        + flux_north
        - jnp.concatenate([flux_west, flux_east[:, :, :, :-1, :]], 3)
        - jnp.concatenate([flux_south, flux_north[:, :, :, :, :-1]], 4)
        + jnp.pad(flux_down, ((0, 0), (0, 0), (0, 1), (0, 0), (0, 0)))
        - jnp.pad(flux_down, ((0, 0), (0, 0), (1, 0), (0, 0), (0, 0)))
    )
    flat_balance = balance_all.reshape(3, 3, -1)
    mob_flat = mob_streams.reshape(3, 3, -1)
    press_flat = press_streams.reshape(3, -1)
    slots = perforation_cell.shape[1]
    peer_most = slots // tiles_x
    slot_iota = jnp.arange(slots, dtype=jnp.int32)
    owner_tile = slot_iota // peer_most
    slot_rank = slot_iota % peer_most
    counts = jnp.broadcast_to(perforation_count[0][:, None], (tiles_x, peer_most)).reshape(slots)
    weight = jnp.where(slot_rank < counts, well_index[0], 0.0)
    slot_cells = perforation_cell[0]
    weighted_mob = weight * mob_flat[:, :, slot_cells]
    cell_press = press_flat[:, slot_cells]
    segment_row = lax.all_gather(seg_streams, "xt", axis=2, tiled=True)
    seg_number = perforation_segment[0]
    slot_index = (
        seg_number // cols_seg * (cols_seg * tiles_x)
        + owner_tile * cols_seg
        + seg_number % cols_seg
    )
    pressure_drop = cell_press - segment_row.reshape(3, -1)[:, slot_index]
    rates_here = dual_product(weighted_mob, pressure_drop[:, None])
    dense_inflow = (
        jnp.zeros((3, rows_seg * cols_seg * tiles_x), jnp.float32)
        .at[:, slot_index]
        .add(rates_here.sum(1))
        .reshape(3, rows_seg, cols_seg * tiles_x)
    )
    inflow = lax.psum_scatter(dense_inflow, "xt", scatter_dimension=2, tiled=True)
    flat_balance = flat_balance.at[:, :, slot_cells].add(rates_here)
    balance_all = flat_balance.reshape(3, 3, layers, width_x, width_y)
    segment_out = inflow - link_flow + jnp.concatenate([carried_in, carried[:, :, :-1]], 2)
    return (balance_all[0], balance_all[1:], segment_out)


def solution(mesh):
    in_specs = (
        P(None, "xt", "yt"),
        P(None, None, "xt", "yt"),
        P(None, None, "xt", "yt"),
        P(None, "xt", "yt"),
        P(None, None, "xt", "yt"),
        P(None, "xt", "yt"),
        P(None, None, None, "xt", "yt"),
        P("yt", "xt"),
        P(None, "yt", "xt"),
        P("yt", "xt"),
        P("yt", "xt"),
        P("yt", "xt"),
        P("yt", "xt"),
        P("yt", "xt"),
        P("yt", "xt"),
        P("yt", "xt"),
    )
    out_specs = (P(None, None, "xt", "yt"), P(None, None, None, "xt", "yt"), P(None, "yt", "xt"))
    return jax.shard_map(body, mesh=mesh, in_specs=in_specs, out_specs=out_specs, check_vma=False)
```

profile of v0, /device:TPU:56, one launch (start us, length us, event | category | flops | bytes accessed | tf_op | source)
XLA Modules:
  0.0 375.1 jit_solution(14823499823405472154)
XLA Ops:
  7.3 1.3 convert_element_type.7
  8.5 1.3 collective-permute-start.6
  9.8 1.3 fusion.75
  11.1 1.3 collective-permute-start.7
  12.4 0.8 bitcast_multiply_fusion.22
  13.2 1.6 fusion.50
  14.8 1.5 fusion.90
  16.4 2.7 collective-permute-start.2
  19.8 1.3 collective-permute-start
  21.1 0.9 slice_bitcast_fusion
  21.9 1.4 fusion.12
  23.3 2.6 collective-permute-start.3
  25.9 1.3 slice.334
  27.2 1.4 fusion.74
  28.6 0.8 fusion.21
  29.6 1.4 fusion.60
  31.0 1.5 fusion.25
  33.3 0.8 fusion.11
  34.2 1.4 fusion.76
  38.9 10.7 %copy.93 = f32[3,3,8192]{1,0,2:T(4,128)} copy(f32[3,3,8192]{2,1,0:T(4,128)S(1)} %pad_maximum_fusion) | data formatting | bytes 589824 | tf_op jit(solution)/shard_map/stack | solution.py:49
  50.2 7.3 %gather_fusion = f32[512,3,3]{2,1,0:T(4,128)S(1)} fusion(f32[3,3,8192]{1,0,2:T(4,128)} %copy.93, s32[1024]{0:T(1024)S(1)} %get-tuple-element.118), kind=kCustom, calls=%fused_computation | custom fusion | bytes 38912 | tf_op jit(solution)/shard_map/gather | solution.py:185
  58.2 2.7 copy.95
  60.8 3.2 gather_fusion.1
  67.7 0.8 maximum_bitcast_fusion.3
  68.6 0.9 add_compare_fusion
  69.5 1.3 collective-permute-start.1
  70.8 0.8 fusion.81
  71.5 0.8 broadcast_select_fusion
  72.4 56.6 %all_gather.3 = f32[3,8,4096]{2,1,0:T(8,128)S(1)} all-gather(f32[3,8,128]{2,1,0:T(8,128)S(1)} %get-tuple-element.105), channel_id=1, replica_groups=mesh['xt'=32,'yt'=16] {'xt'}, dimensions={2}, use_global_device_ids=true | all-gather | bytes 405504 | tf_op jit(solution)/shard_map/all_gather | solution.py:187
  129.0 8.6 %copy.96 = f32[3,8,4096]{0,2,1:T(8,128)} copy(f32[3,8,4096]{2,1,0:T(8,128)S(1)} %all_gather.3) | data formatting | bytes 786432 | tf_op jit(solution)/shard_map/all_gather | solution.py:187
  137.6 6.8 %gather_fusion.2 = f32[512,3]{1,0:T(8,128)S(1)} fusion(f32[3,32768]{0,1:T(8,128)} %bitcast.288, s32[1024]{0:T(1024)S(1)} %copy-done.12), kind=kCustom, calls=%fused_computation.2 | custom fusion | bytes 14336 | tf_op jit(solution)/shard_map/gather | solution.py:194
  145.1 9.1 %scatter_custom_fusion.1 = f32[3,32768]{0,1:T(8,128)} fusion(s32[512]{0:T(512)} %bitcast.334, f32[512,3]{1,0:T(8,128)S(1)} %copy.101, f32[]{:T(128)} %constant.252.clone.1), kind=kCustom, calls=%fused_computation.5 | custom fusion | flops 1536 | bytes 393728 | tf_op jit(solution)/shard_map/scatter-add | solution.py:199
  154.3 10.4 %copy.102 = f32[3,8,4096]{2,1,0:T(8,128)} copy(f32[3,8,4096]{0,2,1:T(8,128)} %bitcast.285) | data formatting | bytes 786432 | tf_op jit(solution)/shard_map/reshape | solution.py:200
  164.7 1.0 maximum_subtract_fusion
  165.8 1.1 maximum_select_fusion
  167.0 0.9 slice.372
  167.8 2.1 collective-permute-start.5
  170.1 3.1 collective-permute-start.4
  173.7 2.1 collective-permute-start.8
  176.8 1.2 fusion.6
  178.0 8.7 %copy.92 = f32[3,3,8,8,128]{1,0,4,3,2:T(4,128)} copy(f32[3,3,8,8,128]{4,3,2,1,0:T(8,128)S(1)} %fusion.6) | data formatting | bytes 589824 | tf_op jit(solution)/shard_map/sub | solution.py:166
  186.7 49.3 %scatter_fusion = f32[3,3,8192]{1,0,2:T(4,128)} fusion(f32[3,3,8192]{1,0,2:T(4,128)} %bitcast.286, s32[512]{0:T(512)S(1)} %bitcast.332, f32[512,3,3]{2,1,0:T(4,128)S(1)} %copy.100), kind=kCustom, calls=%fused_computation.3 | custom fusion | flops 4608 | bytes 57344 | tf_op jit(solution)/shard_map/scatter-add | solution.py:203
  236.0 10.5 %slice.393 = f32[2,3,8192]{1,0,2:T(2,128)} slice(f32[3,3,8192]{1,0,2:T(4,128)} %scatter_fusion), slice={[1:3], [0:3], [0:8192]} | slice | bytes 393216 | tf_op jit(solution)/shard_map/slice | solution.py:206
  246.5 8.6 %slice.392 = f32[1,3,8192]{1,0,2:T(1,128)} slice(f32[3,3,8192]{1,0,2:T(4,128)} %scatter_fusion), slice={[0:1], [0:3], [0:8192]} | slice | bytes 196608 | tf_op jit(solution)/shard_map/slice | solution.py:206
  255.2 7.7 %copy.104 = f32[2,3,8,8,128]{4,3,2,1,0:T(8,128)} copy(f32[2,3,8,8,128]{1,0,4,3,2:T(2,128)} %bitcast.287) | data formatting | bytes 393216
  262.8 3.5 copy.103
  266.3 100.5 %reduce-scatter.2.cloned.1.call-done = f32[3,8,128]{2,1,0:T(8,128)} async-done(((f32[3,8,4096]{2,1,0:T(8,128)}), f32[3,8,128]{2,1,0:T(8,128)}) %reduce-scatter.2.cloned.1.call-update) | async-done | bytes 12304 | tf_op jit(solution)/shard_map/reduce_scatter | solution.py:202
  366.9 1.4 maximum_add_fusion.1
  (99 shorter events, 12.3 us)
Async XLA Ops:
  7.2 50.9 %copy-start = (f32[8,8,128]{2,1,0:T(8,128)S(1)}, f32[8,8,128]{2,1,0:T(8,128)}, u32[]{:S(2)}) copy-start(f32[8,8,128]{2,1,0:T(8,128)} %param.19) | copy-start | bytes 98308
  7.2 56.9 %copy-start.2 = (s32[8,8,128]{2,1,0:T(8,128)S(1)}, s32[8,8,128]{2,1,0:T(8,128)}, u32[]{:S(2)}) copy-start(s32[8,8,128]{2,1,0:T(8,128)} %param.24) | copy-start | bytes 98308
  7.2 42.4 %copy-start.14 = (s32[1,512]{1,0:T(1,128)S(1)}, s32[1,512]{1,0:T(1,128)}, u32[]{:S(2)}) copy-start(s32[1,512]{1,0:T(1,128)} %param.31) | copy-start | bytes 6148
  7.2 42.4 %copy-start.15 = (s32[1,512]{1,0:T(1,128)S(1)}, s32[1,512]{1,0:T(1,128)}, u32[]{:S(2)}) copy-start(s32[1,512]{1,0:T(1,128)} %param.32) | copy-start | bytes 6148
  7.2 61.3 %copy-start.3 = (f32[8,8,128]{2,1,0:T(8,128)S(1)}, f32[8,8,128]{2,1,0:T(8,128)}, u32[]{:S(2)}) copy-start(f32[8,8,128]{2,1,0:T(8,128)} %param.22) | copy-start | bytes 98308
  7.2 359.6 %reduce-scatter.2.cloned.1.call-start = ((), (), s32[]{:S(2)}) async-start(), calls=%async_computation.1 | async-start | bytes 405504 | tf_op jit(solution)/shard_map/reduce_scatter | solution.py:202
  8.5 60.9 %collective-permute-start.6 = (f32[8,1]{1,0:T(8,128)}, f32[8,1]{1,0:T(8,128)}, u32[]{:S(2)}, u32[]{:S(2)}) collective-permute-start(f32[8,1]{1,0:T(8,128)} %bitcast.283), channel_id=1, source_target_pairs={{16,0},{32,16},{48,32},{64,48},{80,64},{96,80},{112,96},{128,112},... | collective-permute-start | bytes 104 | tf_op jit(solution)/shard_map/ppermute | solution.py:14
  11.1 60.4 %collective-permute-start.7 = (f32[3,8,1]{2,1,0:T(8,128)}, f32[3,8,1]{2,1,0:T(8,128)}, u32[]{:S(2)}, u32[]{:S(2)}) collective-permute-start(f32[3,8,1]{2,1,0:T(8,128)} %fusion.75), channel_id=1, source_target_pairs={{16,0},{32,16},{48,32},{64,48},{80,64},{96,80},{112,96},{128,112},... | collective-permute-start | bytes 296 | tf_op jit(solution)/shard_map/ppermute | solution.py:14
  16.4 149.3 %collective-permute-start.2 = (f32[3,3,8,8,1]{4,3,2,1,0:T(8,128)S(1)}, f32[3,3,8,8,1]{4,3,2,1,0:T(8,128)}, u32[]{:S(2)}, u32[]{:S(2)}) collective-permute-start(f32[3,3,8,8,1]{4,3,2,1,0:T(8,128)S(1)} %bitcast.290), channel_id=1, source_target_pairs={{1,0},{2,1},{3,2},{4,3},{5,4},{6,5},{7,6},{8,7},{9,8},{10,9},{11,1... | collective-permute-start | bytes 6920 | tf_op jit(solution)/shard_map/ppermute | solution.py:14
  19.8 146.0 %collective-permute-start = (f32[3,3,8,1,128]{4,3,2,1,0:T(1,128)}, f32[3,3,8,1,128]{4,3,2,1,0:T(1,128)}, u32[]{:S(2)}, u32[]{:S(2)}) collective-permute-start(f32[3,3,8,1,128]{4,3,2,1,0:T(1,128)} %slice.347), channel_id=1, source_target_pairs={{16,0},{32,16},{48,32},{64,48},{80,64},{96,80},{112,96},{128,112},... | collective-permute-start | bytes 110600 | tf_op jit(solution)/shard_map/ppermute | solution.py:14
  23.3 141.4 %collective-permute-start.3 = (f32[3,8,8,1]{3,2,1,0:T(8,128)}, f32[3,8,8,1]{3,2,1,0:T(8,128)}, u32[]{:S(2)}, u32[]{:S(2)}) collective-permute-start(f32[3,8,8,1]{3,2,1,0:T(8,128)} %fusion.12), channel_id=1, source_target_pairs={{1,0},{2,1},{3,2},{4,3},{5,4},{6,5},{7,6},{8,7},{9,8},{10,9},{11,1... | collective-permute-start | bytes 2312 | tf_op jit(solution)/shard_map/ppermute | solution.py:14
  38.5 30.0 %copy-start.4 = (f32[1,8,8,128]{3,2,1,0:T(8,128)S(1)}, f32[1,8,8,128]{3,2,1,0:T(8,128)}, u32[]{:S(2)}) copy-start(f32[1,8,8,128]{3,2,1,0:T(8,128)} %get-tuple-element.73) | copy-start | bytes 98308
  38.8 19.1 %copy-start.18 = (s32[1,32]{1,0:T(1,128)S(1)}, s32[1,32]{1,0:T(1,128)}, u32[]{:S(2)}) copy-start(s32[1,32]{1,0:T(1,128)} %param.34) | copy-start | bytes 388
  38.8 29.7 %copy-start.5 = (f32[1,8,8,128]{3,2,1,0:T(8,128)S(1)}, f32[1,8,8,128]{3,2,1,0:T(8,128)}, u32[]{:S(2)}) copy-start(f32[1,8,8,128]{3,2,1,0:T(8,128)} %get-tuple-element.75) | copy-start | bytes 98308
  38.8 29.7 %copy-start.6 = (f32[8,8,128]{2,1,0:T(8,128)S(1)}, f32[8,8,128]{2,1,0:T(8,128)}, u32[]{:S(2)}) copy-start(f32[8,8,128]{2,1,0:T(8,128)} %get-tuple-element.45) | copy-start | bytes 98308
  38.8 29.7 %copy-start.7 = (f32[8,8,128]{2,1,0:T(8,128)S(1)}, f32[8,8,128]{2,1,0:T(8,128)}, u32[]{:S(2)}) copy-start(f32[8,8,128]{2,1,0:T(8,128)} %get-tuple-element.64) | copy-start | bytes 98308
  38.9 29.7 %copy-start.8 = (f32[1,8,8,128]{3,2,1,0:T(8,128)S(1)}, f32[1,8,8,128]{3,2,1,0:T(8,128)}, u32[]{:S(2)}) copy-start(f32[1,8,8,128]{3,2,1,0:T(8,128)} %get-tuple-element.89) | copy-start | bytes 98308
  49.6 8.3 %copy-start.10 = (s32[512,1]{0,1:T(1,128)}, s32[512,1]{0,1:T(1,128)S(1)}, u32[]{:S(2)}) copy-start(s32[512,1]{0,1:T(1,128)S(1)} %compare_select_fusion.1) | copy-start | bytes 6148
  49.6 8.3 %copy-start.13 = (s32[512,1]{0,1:T(1,128)}, s32[512,1]{0,1:T(1,128)S(1)}, u32[]{:S(2)}) copy-start(s32[512,1]{0,1:T(1,128)S(1)} %compare_select_fusion) | copy-start | bytes 6148
  57.9 79.7 %copy-start.12 = (s32[1024]{0:T(1024)S(1)}, s32[1024]{0:T(1024)}, u32[]{:S(2)}) copy-start(s32[1024]{0:T(1024)} %get-tuple-element.117) | copy-start | bytes 12292
  69.5 95.2 %collective-permute-start.1 = (f32[3,8,1,128]{3,2,1,0:T(1,128)}, f32[3,8,1,128]{3,2,1,0:T(1,128)S(1)}, u32[]{:S(2)}, u32[]{:S(2)}) collective-permute-start(f32[3,8,1,128]{3,2,1,0:T(1,128)} %fusion.76), channel_id=1, source_target_pairs={{16,0},{32,16},{48,32},{64,48},{80,64},{96,80},{112,96},{128,112},... | collective-permute-start | bytes 36872 | tf_op jit(solution)/shard_map/ppermute | solution.py:14
  145.1 21.8 %copy-start.17 = (pred[128]{0:T(512)(128)(4,1)S(1)}, pred[128]{0:T(512)(128)(4,1)}, u32[]{:S(2)}) copy-start(pred[128]{0:T(512)(128)(4,1)} %compare_and_fusion.1) | copy-start | bytes 388
  145.1 24.8 %copy-start.16 = (pred[8]{0:T(512)(128)(4,1)S(1)}, pred[8]{0:T(512)(128)(4,1)}, u32[]{:S(2)}) copy-start(pred[8]{0:T(512)(128)(4,1)} %compare_and_fusion) | copy-start | bytes 28
  154.3 18.9 %copy-start.9 = (f32[3,8,8,128]{3,2,1,0:T(8,128)S(1)}, f32[3,8,8,128]{3,2,1,0:T(8,128)}, u32[]{:S(2)}) copy-start(f32[3,8,8,128]{3,2,1,0:T(8,128)} %param.21) | copy-start | bytes 294916
  164.7 22.0 %copy-start.11 = (s32[512,1]{0,1:T(1,128)S(1)}, s32[512,1]{0,1:T(1,128)}, u32[]{:S(2)}) copy-start(s32[512,1]{0,1:T(1,128)} %copy-done.10) | copy-start | bytes 6148
  167.8 8.2 %collective-permute-start.5 = (f32[3,3,8,8,1]{4,3,2,1,0:T(8,128)}, f32[3,3,8,8,1]{4,3,2,1,0:T(8,128)S(1)}, u32[]{:S(2)}, u32[]{:S(2)}) collective-permute-start(f32[3,3,8,8,1]{4,3,2,1,0:T(8,128)} %slice.372), channel_id=1, source_target_pairs={{0,1},{1,2},{2,3},{3,4},{4,5},{5,6},{6,7},{7,8},{8,9},{9,10},{10,1... | collective-permute-start | bytes 6920 | tf_op jit(solution)/shard_map/ppermute | solution.py:14
  170.1 6.0 %collective-permute-start.4 = (f32[3,3,8,1,128]{4,3,2,1,0:T(1,128)S(1)}, f32[3,3,8,1,128]{4,3,2,1,0:T(1,128)S(1)}, u32[]{:S(2)}, u32[]{:S(2)}) collective-permute-start(f32[3,3,8,1,128]{4,3,2,1,0:T(1,128)S(1)} %slice.370), channel_id=1, source_target_pairs={{0,16},{16,32},{32,48},{48,64},{64,80},{80,96},{96,112},{112,128},... | collective-permute-start | bytes 110600 | tf_op jit(solution)/shard_map/ppermute | solution.py:14
  173.7 92.6 %collective-permute-start.8 = (f32[3,8,1]{2,1,0:T(8,128)S(1)}, f32[3,8,1]{2,1,0:T(8,128)S(1)}, u32[]{:S(2)}, u32[]{:S(2)}) collective-permute-start(f32[3,8,1]{2,1,0:T(8,128)S(1)} %slice.398), channel_id=1, source_target_pairs={{0,16},{16,32},{32,48},{48,64},{64,80},{80,96},{96,112},{112,128},... | collective-permute-start | bytes 296 | tf_op jit(solution)/shard_map/ppermute | solution.py:14
  176.1 0.7 copy-start.1
Sparse Core Ops, SparseCore 0:
  164.8 202.0 reduce-scatter.1
where the time goes:
time: 379 us; the launch traced here: 375 us
  waiting for transfers between devices  101 us (27%)
  local copies, waits for them, and re-layouts  96.5 us (25%)
  other arithmetic  88.9 us (23%)
  blocking collectives  56.6 us (15%)
  starting transfers between devices  17.7 us (5%)
  between operations  14.7 us (4%)
    reduce_scatter x1, waiting for transfers between devices, body(): lax.psum_scatter(dense_inflow, 'xt', scatter_dimension=2, tiled=True)  101 us
    all_gather x1, blocking collectives, body(): segment_row = lax.all_gather(seg_streams, 'xt', axis=2, tiled=True)  56.6 us
    scatter-add x1, other arithmetic, body(): flat_balance = flat_balance.at[:, :, slot_cells].add(rates_here)  49.3 us
    slice x2, local copies, waits for them, and re-layouts, body(): return (balance_all[0], balance_all[1:], segment_out)  19.2 us
    ppermute x9, starting transfers between devices, from_behind(): return lax.ppermute(array, axis, pairs)  17.7 us
    unnamed x44, local copies, waits for them, and re-layouts  12.9 us
    another operation x1, local copies, waits for them, and re-layouts, stream_properties(): return (jnp.stack(mobility_list, 1), jnp.stack(mass_list, 1))  10.7 us
    reshape x1, local copies, waits for them, and re-layouts, body(): dense_inflow = jnp.zeros((3, rows_seg * cols_seg * tiles_x), jnp.float32)...  10.4 us
  transfers between devices with their start and end apart: 10, of which 2 were waited for; matrix products, arithmetic and copies ran while one was open for 48% of the time, Pallas kernels for 0%

commit v1 on v0

v1 whole, which is shorter than its diff:
```python
import jax
import jax.numpy as jnp
from jax import lax
from jax.experimental import pallas as pl
from jax.experimental.pallas import tpu as pltpu
from jax.sharding import PartitionSpec as P

COMPRESS = (0.05, 0.1, 0.6)
INV_VISCOSITY = (2.0, 0.5, 5.0)
GRAVITY_HEAD = (0.3, 0.25, 0.05)

NZ = 8
LANES = 128
CELL_ROWS = 64
SLOTS = 512
TILES = 32
PEER = 16
ROWS_A = 24
F32 = jnp.float32
BF16 = jnp.bfloat16
VMEM = pl.BlockSpec(memory_space=pltpu.VMEM)


def roll(x, shift, axis):
    return pltpu.roll(x, shift % x.shape[axis], axis)


def iota(shape, dim):
    return lax.broadcasted_iota(jnp.int32, shape, dim)


def split(x):
    hi = x.astype(BF16)
    lo = (x - hi.astype(F32)).astype(BF16)
    return hi, lo


def one_hot(mask):
    return jnp.where(mask, 1.0, 0.0).astype(BF16)


def properties(press, water, gas):
    oil = (1.0 - water[0] - gas[0], -water[1] - gas[1], -water[2] - gas[2])
    mobility, mass = [], []
    for phase, sat in enumerate((water, oil, gas)):
        c = COMPRESS[phase]
        base = jnp.exp(c * press[0])
        cb = c * base
        m0 = base * sat[0]
        cs = cb * sat[0]
        m1 = cs * press[1] + base * sat[1]
        m2 = cs * press[2] + base * sat[2]
        v = INV_VISCOSITY[phase]
        vs = v * sat[0]
        vm = v * m0
        mobility.append((m0 * vs, m1 * vs + vm * sat[1], m2 * vs + vm * sat[2]))
        mass.append((m0, m1, m2))
    return mobility, mass


def fluxes(mob_low, mob_up, press_low, press_up, trans, code, direction, heads):
    drop = [trans * (press_low[s] - press_up[s]) for s in range(3)]
    out = []
    for phase in range(3):
        bit = (code & (1 << (3 * direction + phase))) != 0
        up = [jnp.where(bit, mob_up[phase][s], mob_low[phase][s]) for s in range(3)]
        first = drop[0] if heads is None else drop[0] + trans * heads[phase]
        out.append(
            (
                up[0] * first,
                up[1] * first + up[0] * drop[1],
                up[2] * first + up[0] * drop[2],
            )
        )
    return out


def nine(p_ref, s_ref, ct_ref, at):
    return [
        p_ref[at, :], ct_ref[0, 0, at, :], ct_ref[1, 0, at, :],
        s_ref[0, at, :], ct_ref[0, 1, at, :], ct_ref[1, 1, at, :],
        s_ref[1, at, :], ct_ref[0, 2, at, :], ct_ref[1, 2, at, :],
    ]


def slot_kernel(p_ref, s_ref, ct_ref, sp_ref, st_ref, pc_ref, ps_ref, wi_ref, cnt_ref, pay_ref, slot_ref):
    at = pl.ds(0, CELL_ROWS)
    hi, lo = split(jnp.concatenate(nine(p_ref, s_ref, ct_ref, at), 0))
    raw = jnp.concatenate([hi, lo], 1)
    cell = pc_ref[...]
    lane = cell & (LANES - 1)
    row = cell >> 7
    lane_hot = one_hot(iota((LANES, SLOTS), 0) == lane)
    picked = jnp.dot(raw, jnp.concatenate([lane_hot, lane_hot], 0), preferred_element_type=F32)
    row_mask = iota((CELL_ROWS, SLOTS), 0) == row
    val = [
        jnp.sum(jnp.where(row_mask, picked[q * CELL_ROWS:(q + 1) * CELL_ROWS], 0.0), axis=0, keepdims=True)
        for q in range(9)
    ]
    owner = iota((TILES, SLOTS), 1) >> 4
    tile_hot = one_hot(iota((TILES, SLOTS), 0) == owner)
    counts = jnp.broadcast_to(cnt_ref[...].astype(F32).astype(BF16), (8, TILES))
    live = jnp.dot(counts, tile_hot, preferred_element_type=F32)[0:1]
    rank = (iota((1, SLOTS), 1) & (PEER - 1)).astype(F32)
    weight = jnp.where(rank < live, wi_ref[...], 0.0)
    press = val[0:3]
    mobility, _ = properties(press, val[3:6], val[6:9])
    wl = [[weight * mobility[a][s] for s in range(3)] for a in range(3)]
    total = [wl[0][s] + wl[1][s] + wl[2][s] for s in range(3)]
    carry = [
        total[0] * press[0],
        total[1] * press[0] + total[0] * press[1],
        total[2] * press[0] + total[0] * press[2],
    ]
    slot_ref[...] = jnp.concatenate(
        press + [wl[a][s] for s in range(3) for a in range(3)] + [jnp.zeros((4, SLOTS), F32)], 0
    )
    sent = jnp.concatenate(
        [ps_ref[...].astype(F32)] + carry + total + [jnp.zeros((1, SLOTS), F32)], 0
    )
    seg = [sp_ref[...], st_ref[0], st_ref[1]]
    for k in range(TILES):
        w = k // 8
        for s in range(3):
            pay_ref[k, s * 8:(s + 1) * 8, :] = seg[s]
        pay_ref[k, ROWS_A:ROWS_A + 8, :] = sent[:, w * LANES:(w + 1) * LANES]


def pack_kernel(p_ref, s_ref, ct_ref, t_ref, code_ref, well_ref, link_ref, xlo_ref, xhi_ref, ylo_ref, yhi_ref):
    first, last = pl.ds(0, NZ, stride=8), pl.ds(7, NZ, stride=8)
    for q, v in enumerate(nine(p_ref, s_ref, ct_ref, first)):
        xlo_ref[q * 8:(q + 1) * 8, :] = v
    for q, v in enumerate(nine(p_ref, s_ref, ct_ref, last)):
        xhi_ref[q * 8:(q + 1) * 8, :] = v
    well = well_ref[...].astype(F32)
    xlo_ref[72:80, :] = well
    xhi_ref[72:80, :] = t_ref[0, last, :]
    xhi_ref[80:88, :] = code_ref[last, :].astype(F32)
    xhi_ref[88:96, :] = well
    xhi_ref[96:104, :] = link_ref[...]
    lane = iota((8, LANES), 1)
    low = jnp.zeros((8, LANES), F32)
    high = jnp.zeros((8, LANES), F32)
    for z in range(NZ):
        at = pl.ds(z * 8, 8)
        for q, v in enumerate(nine(p_ref, s_ref, ct_ref, at)):
            c = q * 8 + z
            low = jnp.where(lane == c, roll(v, c, 1), low)
            high = jnp.where(lane == c, roll(v, c + 1, 1), high)
        high = jnp.where(lane == 72 + z, roll(t_ref[1, at, :], 73 + z, 1), high)
        high = jnp.where(lane == 80 + z, roll(code_ref[at, :].astype(F32), 81 + z, 1), high)
    ylo_ref[...] = low
    yhi_ref[...] = high


def stencil_kernel(p_ref, s_ref, ct_ref, om_ref, pv_ref, t_ref, code_ref, ylo_ref, yhi_ref,
                   exlo_ref, wxhi_ref, nylo_ref, syhi_ref, res_ref, prod_ref):
    top_x = lax.axis_index("xt") == TILES - 1
    top_y = lax.axis_index("yt") == lax.axis_size("yt") - 1
    lane = iota((8, LANES), 1)
    sub = iota((8, LANES), 0)

    half = lane < 64
    own_lo, own_hi, north, south = ylo_ref[...], yhi_ref[...], nylo_ref[...], syhi_ref[...]
    low = [jnp.where(half, roll(own_hi, -8 * q, 1), roll(south, 64 - 8 * q, 1)) for q in range(11)]
    up = [jnp.where(half, roll(north, -8 * q, 1), roll(own_lo, 64 - 8 * q, 1)) for q in range(9)]
    code_y = low[10].astype(jnp.int32)
    trans_y = jnp.where(jnp.logical_and(half, top_y), 0.0, low[9])
    rim = fluxes(
        properties(low[0:3], low[3:6], low[6:9])[0], properties(up[0:3], up[3:6], up[6:9])[0],
        low[0:3], up[0:3], trans_y, code_y, 1, None,
    )
    even = (lane & 1) == 0
    edge = jnp.logical_or(lane == 0, lane == LANES - 1)
    rim_even, rim_odd = [], []
    for a in range(3):
        moved = [roll(rim[a][s], 65, 1) for s in range(3)]
        rim_even.append([jnp.where(even, rim[a][s], -moved[s]) for s in range(3)])
        rim_odd.append([jnp.where(even, -moved[s], rim[a][s]) for s in range(3)])

    def put(s, a, at, value):
        if s == 0:
            res_ref[a, at, :] = value
        else:
            prod_ref[s - 1, a, at, :] = value

    def take(s, a, at):
        return res_ref[a, at, :] if s == 0 else prod_ref[s - 1, a, at, :]

    raw = nine(p_ref, s_ref, ct_ref, pl.ds(0, 8))
    mob, mass = properties(raw[0:3], raw[3:6], raw[6:9])
    press = raw[0:3]
    above = None
    for z in range(NZ):
        at = pl.ds(z * 8, 8)
        code = code_ref[at, :]
        volume = pv_ref[at, :]
        bal = [[volume * mass[a][s] for s in range(3)] for a in range(3)]
        for a in range(3):
            bal[a][0] = bal[a][0] - om_ref[a, at, :]
        for direction, axis, last in ((0, 0, sub == 7), (1, 1, lane == LANES - 1)):
            trans = jnp.where(last, 0.0, t_ref[direction, at, :])
            up_mob = [[roll(mob[a][s], -1, axis) for s in range(3)] for a in range(3)]
            up_press = [roll(press[s], -1, axis) for s in range(3)]
            flux = fluxes(mob, up_mob, press, up_press, trans, code, direction, None)
            for a in range(3):
                for s in range(3):
                    bal[a][s] = bal[a][s] + (flux[a][s] - roll(flux[a][s], 1, axis))
        rim_z = rim_even if z % 2 == 0 else rim_odd
        for a in range(3):
            for s in range(3):
                bal[a][s] = bal[a][s] + jnp.where(edge, roll(rim_z[a][s], LANES - 1 - z, 1), 0.0)
        if above is not None:
            for a in range(3):
                for s in range(3):
                    bal[a][s] = bal[a][s] - above[a][s]
        if z < NZ - 1:
            raw = nine(p_ref, s_ref, ct_ref, pl.ds(z * 8 + 8, 8))
            mob_next, mass = properties(raw[0:3], raw[3:6], raw[6:9])
            above = fluxes(mob, mob_next, press, raw[0:3], t_ref[2, at, :], code, 2, GRAVITY_HEAD)
            for a in range(3):
                for s in range(3):
                    bal[a][s] = bal[a][s] + above[a][s]
            mob, press = mob_next, raw[0:3]
        for a in range(3):
            for s in range(3):
                put(s, a, at, bal[a][s])

    first, last = pl.ds(0, NZ, stride=8), pl.ds(7, NZ, stride=8)

    def face(low, up, trans, code):
        return fluxes(
            properties(low[0:3], low[3:6], low[6:9])[0], properties(up[0:3], up[3:6], up[6:9])[0],
            low[0:3], up[0:3], trans, code, 0, None,
        )

    east = [exlo_ref[q * 8:(q + 1) * 8, :] for q in range(9)]
    flux = face(nine(p_ref, s_ref, ct_ref, last), east, jnp.where(top_x, 0.0, t_ref[0, last, :]), code_ref[last, :])
    for a in range(3):
        for s in range(3):
            put(s, a, last, take(s, a, last) + flux[a][s])
    west = [wxhi_ref[q * 8:(q + 1) * 8, :] for q in range(11)]
    flux = face(west[0:9], nine(p_ref, s_ref, ct_ref, first), west[9], west[10].astype(jnp.int32))
    for a in range(3):
        for s in range(3):
            put(s, a, first, take(s, a, first) - flux[a][s])


def join_kernel(got_ref, slot_ref, pc_ref, ps_ref, sp_ref, st_ref, well_ref, link_ref, heel_ref, exlo_ref, wxhi_ref,
                res_in, prod_in, res_ref, prod_ref, seg_ref):
    here = lax.axis_index("xt")
    lane = iota((8, LANES), 1)
    group = iota((1, LANES), 1) >> 4

    seg_number = ps_ref[...]
    seg_lane = seg_number & (LANES - 1)
    seg_row = seg_number >> 7
    rates = [[] for _ in range(9)]
    for w in range(4):
        cols = slice(w * LANES, (w + 1) * LANES)
        hot = one_hot(iota((LANES, LANES), 0) == seg_lane[:, cols])
        hi, lo = split(got_ref[w * 8:(w + 1) * 8, 0:ROWS_A, :].reshape(8 * ROWS_A, LANES))
        picked = jnp.dot(
            jnp.concatenate([hi, lo], 1), jnp.concatenate([hot, hot], 0), preferred_element_type=F32
        ).reshape(8, ROWS_A, LANES)
        mine = jnp.where(group == 0, picked[0], 0.0)
        for k in range(1, 8):
            mine = jnp.where(group == k, picked[k], mine)
        row_mask = iota((8, LANES), 0) == seg_row[:, cols]
        at_seg = [
            jnp.sum(jnp.where(row_mask, mine[s * 8:(s + 1) * 8], 0.0), axis=0, keepdims=True) for s in range(3)
        ]
        drop = [slot_ref[s:s + 1, cols] - at_seg[s] for s in range(3)]
        base = [slot_ref[3 + a:4 + a, cols] for a in range(3)]
        for a in range(3):
            rates[a].append(base[a] * drop[0])
            for s in (1, 2):
                r = 3 + s * 3 + a
                rates[s * 3 + a].append(slot_ref[r:r + 1, cols] * drop[0] + base[a] * drop[s])

    cell = pc_ref[...]
    lane_hot = one_hot(iota((LANES, SLOTS), 0) == (cell & (LANES - 1)))
    row_hot = one_hot(iota((CELL_ROWS, SLOTS), 0) == (cell >> 7))
    parts = [split(jnp.concatenate(r, 1)) for r in rates]
    left = jnp.concatenate(
        [jnp.concatenate([row_hot * hi, row_hot * lo], 1) for hi, lo in parts], 0
    )
    added = lax.dot_general(
        left, jnp.concatenate([lane_hot, lane_hot], 1), (((1,), (1,)), ((), ())), preferred_element_type=F32
    )
    for s in range(3):
        for a in range(3):
            n = s * 3 + a
            more = added[n * CELL_ROWS:(n + 1) * CELL_ROWS]
            if s == 0:
                res_ref[a] = res_in[a] + more
            else:
                prod_ref[s - 1, a] = prod_in[s - 1, a] + more

    turn = here & 7
    windows = []
    for w in range(4):
        acc = jnp.zeros((8, LANES), F32)
        for k in range(8):
            tile = got_ref[w * 8 + k, ROWS_A:ROWS_A + 8, :]
            shift = ((k - turn + 8) & 7) * PEER
            acc = jnp.where(group == k, pltpu.roll(tile, shift, 1), acc)
        windows.append(acc)
    told = jnp.concatenate(windows, 1)
    number = told[0:1].astype(jnp.int32)
    hot = one_hot(iota((LANES, SLOTS), 0) == (number & (LANES - 1)))
    row_mask = iota((8, SLOTS), 0) == (number >> 7)
    hi, lo = split(jnp.concatenate([jnp.where(row_mask, told[q:q + 1], 0.0) for q in range(1, 7)], 0))
    sums = lax.dot_general(
        jnp.concatenate([hi, lo], 1), jnp.concatenate([hot, hot], 1), (((1,), (1,)), ((), ())),
        preferred_element_type=F32,
    )
    c = [sums[s * 8:(s + 1) * 8] for s in range(3)]
    a = [sums[24 + s * 8:32 + s * 8] for s in range(3)]
    seg = [sp_ref[...], st_ref[0], st_ref[1]]
    inflow = [
        c[0] - seg[0] * a[0],
        c[1] - seg[0] * a[1] - seg[1] * a[0],
        c[2] - seg[0] * a[2] - seg[2] * a[0],
    ]

    after, before = (here + 1) % TILES, (here + TILES - 1) % TILES
    well = well_ref[...].astype(F32)
    link = link_ref[...]
    lane0 = lane == 0
    next_well = roll(jnp.where(lane0, exlo_ref[72:80, :], well), -1, 1)
    linked = jnp.logical_and(
        next_well == well, jnp.logical_not(jnp.logical_and(here == TILES - 1, lane == LANES - 1))
    )
    joined = jnp.logical_and(roll(wxhi_ref[88:96, :], 1, 1) == well, here > 0)
    link_west = roll(wxhi_ref[96:104, :], 1, 1)
    east = got_ref[after, 0:ROWS_A, :]
    west = got_ref[before, 0:ROWS_A, :]
    for s in range(3):
        part = slice(s * 8, (s + 1) * 8)
        next_press = roll(jnp.where(lane0, east[part], seg[s]), -1, 1)
        end = heel_ref[...] if s == 0 else jnp.zeros((8, LANES), F32)
        flow = link * (seg[s] - jnp.where(linked, next_press, end))
        carried = jnp.where(linked, flow, 0.0)
        entering = jnp.where(joined, link_west * (roll(west[part], 1, 1) - seg[s]), 0.0)
        seg_ref[s] = inflow[s] - flow + jnp.where(lane0, entering, roll(carried, 1, 1))


def call(kernel, out_shapes, *args, **kw):
    return pl.pallas_call(
        kernel,
        out_shape=[jax.ShapeDtypeStruct(s, F32) for s in out_shapes],
        in_specs=[VMEM] * len(args),
        out_specs=[VMEM] * len(out_shapes),
        compiler_params=pltpu.CompilerParams(vmem_limit_bytes=40 * 2**20),
        **kw,
    )(*args)


def shift(array, axis, by):
    length = lax.axis_size(axis)
    return lax.ppermute(array, axis, [(i, i + by) for i in range(length) if 0 <= i + by < length])


def body(
    pressure, saturation, old_mass, pore_volume, transmissibility, upwind_code, cell_tangent, segment_pressure,
    segment_tangent, segment_well, link_factor, heel_pressure, perforation_cell, perforation_segment, well_index,
    perforation_count,
):
    p = pressure.reshape(CELL_ROWS, LANES)
    sat = saturation.reshape(2, CELL_ROWS, LANES)
    om = old_mass.reshape(3, CELL_ROWS, LANES)
    pv = pore_volume.reshape(CELL_ROWS, LANES)
    tr = transmissibility.reshape(3, CELL_ROWS, LANES)
    code = upwind_code.reshape(CELL_ROWS, LANES)
    ct = cell_tangent.reshape(2, 3, CELL_ROWS, LANES)

    pay, slots = call(
        slot_kernel, [(TILES, 32, LANES), (16, SLOTS)],
        p, sat, ct, segment_pressure, segment_tangent, perforation_cell, perforation_segment, well_index,
        perforation_count,
    )
    got = lax.all_to_all(pay, "xt", 0, 0, tiled=True)
    xlo, xhi, ylo, yhi = call(
        pack_kernel, [(80, LANES), (104, LANES), (8, LANES), (8, LANES)],
        p, sat, ct, tr, code, segment_well, link_factor,
    )
    east_xlo = shift(xlo, "xt", -1)
    west_xhi = shift(xhi, "xt", 1)
    north_ylo = shift(ylo, "yt", -1)
    south_yhi = shift(yhi, "yt", 1)
    res, prod = call(
        stencil_kernel, [(3, CELL_ROWS, LANES), (2, 3, CELL_ROWS, LANES)],
        p, sat, ct, om, pv, tr, code, ylo, yhi, east_xlo, west_xhi, north_ylo, south_yhi,
    )
    res, prod, seg = call(
        join_kernel, [(3, CELL_ROWS, LANES), (2, 3, CELL_ROWS, LANES), (3, 8, LANES)],
        got, slots, perforation_cell, perforation_segment, segment_pressure, segment_tangent, segment_well,
        link_factor, heel_pressure, east_xlo, west_xhi, res, prod,
        input_output_aliases={11: 0, 12: 1},
    )
    return (res.reshape(old_mass.shape), prod.reshape(cell_tangent.shape), seg)


def solution(mesh):
    cell, seg = P(None, "xt", "yt"), P("yt", "xt")
    cell2, cell3, seg2 = P(None, None, "xt", "yt"), P(None, None, None, "xt", "yt"), P(None, "yt", "xt")
    in_specs = (
        cell, cell2, cell2, cell, cell2, cell, cell3, seg, seg2, seg, seg, seg, seg, seg, seg, seg,
    )
    return jax.shard_map(body, mesh=mesh, in_specs=in_specs, out_specs=(cell2, cell3, seg2), check_vma=False)
```

time: 379 us -> 43.1 us (0.11)
  waiting for transfers between devices: 101 us -> 7 us
  local copies, waits for them, and re-layouts: 96.5 us -> 6.68 us
  other arithmetic: 88.9 us -> 0 us
  blocking collectives: 56.6 us -> 0 us
  between operations: 14.7 us -> 0.85 us
  Pallas kernels: 0 us -> 5.28 us
  starting transfers between devices: 17.7 us -> 22.6 us
    reduce_scatter x1 -> x0, waiting for transfers between devices: 101 us -> none  [body(): lax.psum_scatter(dense_inflow, 'xt', scatter_dimension=2, tiled=True)]
    scatter-add x2 -> x0, other arithmetic: 58.5 us -> none  [the longest x1 49.3 us: body(): flat_balance = flat_balance.at[:, :, slot_cells].add(rates_here)]
    all_gather x1 -> x0, blocking collectives: 56.6 us -> none  [body(): segment_row = lax.all_gather(seg_streams, 'xt', axis=2, tiled=True)]
    slice x10 -> x0, local copies, waits for them, and re-layouts: 22.7 us -> none  [the longest x2 19.2 us: body(): return (balance_all[0], balance_all[1:], segment_out)]
    gather x4 -> x0, local copies, waits for them, and re-layouts: 17.6 us -> none  [the longest x2 7.63 us: body(): weighted_mob = weight * mob_flat[:, :, slot_cells]]
    all_to_all x0 -> x1, starting transfers between devices: none -> 13.3 us  [body(): got = lax.all_to_all(pay, 'xt', 0, 0, tiled=True)]
    another operation x3 -> x0, local copies, waits for them, and re-layouts: 11.1 us -> none  [the longest x1 10.7 us: stream_properties(): return (jnp.stack(mobility_list, 1), jnp.stack(mass_list, 1))]
    reshape x2 -> x0, local copies, waits for them, and re-layouts: 10.5 us -> none  [the longest x1 10.4 us: body(): dense_inflow = jnp.zeros((3, rows_seg * cols_seg * tiles_x), jnp.float32)...]
  transfers between devices with their start and end apart: 10 -> 5, of which waited for: 2 -> 2; matrix products, arithmetic and copies ran while one was open for 48% -> 0% of each run, Pallas kernels for 0% -> 4%
where the time goes in v1:
time: 43.1 us; the launch traced here: 42.4 us
  starting transfers between devices  22.6 us (52%)
  waiting for transfers between devices  7 us (16%)
  local copies, waits for them, and re-layouts  6.68 us (15%)
  Pallas kernels  5.28 us (12%)
  between operations  0.85 us (2%)
    all_to_all x1, starting transfers between devices, body(): got = lax.all_to_all(pay, 'xt', 0, 0, tiled=True)  13.3 us
    ppermute x4, starting transfers between devices, shift(): lax.ppermute(array, axis, [(i, i + by) for i in range(length) if 0 <= i +...  9.31 us
    unnamed x44, local copies, waits for them, and re-layouts  6.68 us
    pallas_call x4, Pallas kernels, call(): pl.pallas_call(kernel, out_shape=[jax.ShapeDtypeStruct(s, F32) for s in o...  5.28 us
    all_to_all x1, waiting for transfers between devices, body(): got = lax.all_to_all(pay, 'xt', 0, 0, tiled=True)  4.49 us
    ppermute x4, waiting for transfers between devices, shift(): lax.ppermute(array, axis, [(i, i + by) for i in range(length) if 0 <= i +...  2.51 us
  transfers between devices with their start and end apart: 5, of which 2 were waited for; matrix products, arithmetic and copies ran while one was open for 0% of the time, Pallas kernels for 4%

profile of v1, /device:TPU:56, one launch (start us, length us, event | category | flops | bytes accessed | tf_op | source)
XLA Modules:
  0.0 42.4 jit_solution(4428540141641559806)
XLA Ops:
  0.6 0.0 copy-start.12
  0.6 0.0 copy-start.21
  0.7 0.7 %copy-done.12 = f32[8,128]{1,0:T(8,128)S(1)} copy-done((f32[8,128]{1,0:T(8,128)S(1)}, f32[8,128]{1,0:T(8,128)}, u32[]{:S(2)}) %copy-start.12) | copy-done | bytes 4120
  1.3 0.0 copy-done.21
  1.3 0.0 copy-start
  1.3 0.9 %copy-done = f32[2,3,8,8,128]{4,3,2,1,0:T(8,128)S(1)} copy-done((f32[2,3,8,8,128]{4,3,2,1,0:T(8,128)S(1)}, f32[2,3,8,8,128]{4,3,2,1,0:T(8,128)}, u32[]{:S(2)}) %copy-start) | copy-done | bytes 196632
  2.2 0.0 copy-start.2
  2.3 0.8 %copy-done.2 = f32[2,8,8,128]{3,2,1,0:T(8,128)S(1)} copy-done((f32[2,8,8,128]{3,2,1,0:T(8,128)S(1)}, f32[2,8,8,128]{3,2,1,0:T(8,128)}, u32[]{:S(2)}) %copy-start.2) | copy-done | bytes 65560
  3.1 0.0 copy-start.5
  3.1 0.8 %copy-done.5 = f32[8,8,128]{2,1,0:T(8,128)S(1)} copy-done((f32[8,8,128]{2,1,0:T(8,128)S(1)}, f32[8,8,128]{2,1,0:T(8,128)}, u32[]{:S(2)}) %copy-start.5) | copy-done | bytes 32792
  3.9 0.7 %copy-done.9 = f32[2,8,128]{2,1,0:T(8,128)S(1)} copy-done((f32[2,8,128]{2,1,0:T(8,128)S(1)}, f32[2,8,128]{2,1,0:T(8,128)}, u32[]{:S(2)}) %copy-start.9) | copy-done | bytes 8216
  4.5 0.7 %copy-done.15 = s32[1,512]{1,0:T(1,128)S(1)} copy-done((s32[1,512]{1,0:T(1,128)S(1)}, s32[1,512]{1,0:T(1,128)}, u32[]{:S(2)}) %copy-start.15) | copy-done | bytes 2072
  5.2 0.7 %copy-done.17 = s32[1,512]{1,0:T(1,128)S(1)} copy-done((s32[1,512]{1,0:T(1,128)S(1)}, s32[1,512]{1,0:T(1,128)}, u32[]{:S(2)}) %copy-start.17) | copy-done | bytes 2072
  5.9 0.7 %copy-done.20 = f32[1,512]{1,0:T(1,128)S(1)} copy-done((f32[1,512]{1,0:T(1,128)S(1)}, f32[1,512]{1,0:T(1,128)}, u32[]{:S(2)}) %copy-start.20) | copy-done | bytes 2072
  6.6 1.2 %shard_map.175 = (f32[32,32,128]{2,1,0:T(8,128)}, f32[16,512]{1,0:T(8,128)S(1)}) custom-call(f32[64,128]{1,0:T(8,128)S(1)} %bitcast.17, f32[2,64,128]{2,1,0:T(8,128)S(1)} %bitcast.12, f32[2,3,64,128]{3,2,1,0:T(8,128)S(1)} %bitcast.9, f32[8,128]{1,0:T(8,128)S(1)} %copy-done.12, f32[2,8,128]{2,1,0:T(8,128)S(1)} %copy-done.9, s32[1,512]{1,0:T(1,128)S(1)} %copy-done.15, ...), custom_call_target="tpu_custom_call" | custom-call | tf_op jit(solution)/shard_map/pallas_call | solution.py:350
  7.8 0.0 copy-start.7
  7.8 0.0 copy-start.13
  7.9 0.0 copy-start.14
  7.9 13.3 %all-to-all-start = ((f32[32,32,128]{2,1,0:T(8,128)}), f32[32,32,128]{2,1,0:T(8,128)S(1)}, u32[]{:S(2)}, u32[]{:S(2)}) async-start(f32[32,32,128]{2,1,0:T(8,128)} %get-tuple-element.14), calls=%async_computation | async-start | bytes 1048576 | tf_op jit(solution)/shard_map/all_to_all | solution.py:383
  21.2 0.0 copy-done.1
  21.2 0.0 copy-done.3
  21.2 0.0 copy-done.4
  21.2 0.0 copy-done.6
  21.2 0.0 copy-done.7
  21.2 0.0 copy-done.13
  21.2 0.0 copy-done.14
  21.3 0.0 copy-start.8
  21.3 0.0 copy-start.11
  21.3 0.2 shard_map.176
  21.5 3.7 %collective-permute-start.1 = (f32[104,128]{1,0:T(8,128)S(1)}, f32[104,128]{1,0:T(8,128)S(1)}, u32[]{:S(2)}, u32[]{:S(2)}) collective-permute-start(f32[104,128]{1,0:T(8,128)S(1)} %get-tuple-element.17), channel_id=1, source_target_pairs={{0,16},{16,32},{32,48},{48,64},{64,80},{80,96},{96,112},{112,128},... | collective-permute-start | bytes 159752 | tf_op jit(solution)/shard_map/ppermute | solution.py:362
  25.2 1.3 %collective-permute-start = (f32[80,128]{1,0:T(8,128)S(1)}, f32[80,128]{1,0:T(8,128)S(1)}, u32[]{:S(2)}, u32[]{:S(2)}) collective-permute-start(f32[80,128]{1,0:T(8,128)S(1)} %get-tuple-element.16), channel_id=1, source_target_pairs={{16,0},{32,16},{48,32},{64,48},{80,64},{96,80},{112,96},{128,112},... | collective-permute-start | bytes 122888 | tf_op jit(solution)/shard_map/ppermute | solution.py:362
  26.5 1.9 %collective-permute-start.2 = (f32[8,128]{1,0:T(8,128)S(1)}, f32[8,128]{1,0:T(8,128)S(1)}, u32[]{:S(2)}, u32[]{:S(2)}) collective-permute-start(f32[8,128]{1,0:T(8,128)S(1)} %get-tuple-element.18.ylo_ref), channel_id=1, source_target_pairs={{1,0},{2,1},{3,2},{4,3},{5,4},{6,5},{7,6},{8,7},{9,8},{10,9},{11,1... | collective-permute-start | bytes 12296 | tf_op jit(solution)/shard_map/ppermute | solution.py:362
  28.5 2.4 %collective-permute-start.3 = (f32[8,128]{1,0:T(8,128)S(1)}, f32[8,128]{1,0:T(8,128)S(1)}, u32[]{:S(2)}, u32[]{:S(2)}) collective-permute-start(f32[8,128]{1,0:T(8,128)S(1)} %get-tuple-element.19.yhi_ref), channel_id=1, source_target_pairs={{0,1},{1,2},{2,3},{3,4},{4,5},{5,6},{6,7},{7,8},{8,9},{9,10},{10,1... | collective-permute-start | bytes 12296 | tf_op jit(solution)/shard_map/ppermute | solution.py:362
  30.9 0.0 collective-permute-done.2.nylo_ref
  30.9 2.5 %collective-permute-done.3.syhi_ref = f32[8,128]{1,0:T(8,128)S(1)} collective-permute-done((f32[8,128]{1,0:T(8,128)S(1)}, f32[8,128]{1,0:T(8,128)S(1)}, u32[]{:S(2)}, u32[]{:S(2)}) %collective-permute-start.3) | collective-permute-done | bytes 4128 | tf_op jit(solution)/shard_map/ppermute | solution.py:362
  33.4 0.0 collective-permute-done.exlo_ref
  33.4 0.0 collective-permute-done.1.wxhi_ref
  33.4 0.0 copy-done.8
  33.4 0.0 copy-done.11
  33.4 0.0 copy-start.10
  33.4 0.0 copy-start.19
  33.4 1.4 %shard_map.177 = (f32[3,64,128]{2,1,0:T(8,128)}, f32[2,3,64,128]{3,2,1,0:T(8,128)}) custom-call(f32[64,128]{1,0:T(8,128)S(1)} %bitcast.19, f32[2,64,128]{2,1,0:T(8,128)S(1)} %bitcast.14, f32[2,3,64,128]{3,2,1,0:T(8,128)S(1)} %bitcast.11, f32[3,64,128]{2,1,0:T(8,128)S(1)} %bitcast.22, f32[64,128]{1,0:T(8,128)S(1)} %bitcast.23, f32[3,64,128]{2,1,0:T(8,128)S(1)} %bitcast.16, ...), custom_call_target="tpu_custom_call" | custom-call | tf_op jit(solution)/shard_map/pallas_call | solution.py:350
  34.9 4.5 %all-to-all-done.got_ref = f32[32,32,128]{2,1,0:T(8,128)S(1)} async-done(((f32[32,32,128]{2,1,0:T(8,128)}), f32[32,32,128]{2,1,0:T(8,128)S(1)}, u32[]{:S(2)}, u32[]{:S(2)}) %all-to-all-start) | async-done | bytes 524320 | tf_op jit(solution)/shard_map/all_to_all | solution.py:383
  39.4 0.0 copy-done.10
  39.4 0.0 copy-done.19
  39.4 0.7 %copy-done.18 = s32[1,512]{1,0:T(1,128)S(1)} copy-done((s32[1,512]{1,0:T(1,128)S(1)}, s32[1,512]{1,0:T(1,128)}, u32[]{:S(2)}) %copy-start.18) | copy-done | bytes 2072
  40.0 0.0 copy-done.16
  40.0 2.4 %shard_map.178 = (f32[3,64,128]{2,1,0:T(8,128)}, f32[2,3,64,128]{3,2,1,0:T(8,128)}, f32[3,8,128]{2,1,0:T(8,128)}) custom-call(f32[32,32,128]{2,1,0:T(8,128)S(1)} %all-to-all-done.got_ref, f32[16,512]{1,0:T(8,128)S(1)} %get-tuple-element.15.slot_ref, s32[1,512]{1,0:T(1,128)S(1)} %copy-done.16, ...), custom_call_target="tpu_custom_call", output_to_operand_aliasing={{0}: (11, {}), {1}: (12, {})} | custom-call | tf_op jit(solution)/shard_map/pallas_call | solution.py:350
  (10 shorter events, 0.0 us)
Async XLA Ops:
  0.6 0.7 %copy-start.12 = (f32[8,128]{1,0:T(8,128)S(1)}, f32[8,128]{1,0:T(8,128)}, u32[]{:S(2)}) copy-start(f32[8,128]{1,0:T(8,128)} %sp_ref.3) | copy-start | bytes 12292
  0.6 0.7 %copy-start.21 = (s32[1,32]{1,0:T(1,128)S(1)}, s32[1,32]{1,0:T(1,128)}, u32[]{:S(2)}) copy-start(s32[1,32]{1,0:T(1,128)} %cnt_ref.1) | copy-start | bytes 388
  1.3 0.9 %copy-start = (f32[2,3,8,8,128]{4,3,2,1,0:T(8,128)S(1)}, f32[2,3,8,8,128]{4,3,2,1,0:T(8,128)}, u32[]{:S(2)}) copy-start(f32[2,3,8,8,128]{4,3,2,1,0:T(8,128)} %param.22) | copy-start | bytes 589828
  2.2 0.8 %copy-start.2 = (f32[2,8,8,128]{3,2,1,0:T(8,128)S(1)}, f32[2,8,8,128]{3,2,1,0:T(8,128)}, u32[]{:S(2)}) copy-start(f32[2,8,8,128]{3,2,1,0:T(8,128)} %param.17) | copy-start | bytes 196612
  3.1 0.8 %copy-start.5 = (f32[8,8,128]{2,1,0:T(8,128)S(1)}, f32[8,8,128]{2,1,0:T(8,128)}, u32[]{:S(2)}) copy-start(f32[8,8,128]{2,1,0:T(8,128)} %param.16) | copy-start | bytes 98308
  3.8 0.7 %copy-start.9 = (f32[2,8,128]{2,1,0:T(8,128)S(1)}, f32[2,8,128]{2,1,0:T(8,128)}, u32[]{:S(2)}) copy-start(f32[2,8,128]{2,1,0:T(8,128)} %st_ref.3) | copy-start | bytes 24580
  4.5 0.7 %copy-start.15 = (s32[1,512]{1,0:T(1,128)S(1)}, s32[1,512]{1,0:T(1,128)}, u32[]{:S(2)}) copy-start(s32[1,512]{1,0:T(1,128)} %pc_ref.3) | copy-start | bytes 6148
  5.2 0.7 %copy-start.17 = (s32[1,512]{1,0:T(1,128)S(1)}, s32[1,512]{1,0:T(1,128)}, u32[]{:S(2)}) copy-start(s32[1,512]{1,0:T(1,128)} %ps_ref.3) | copy-start | bytes 6148
  5.9 0.7 %copy-start.20 = (f32[1,512]{1,0:T(1,128)S(1)}, f32[1,512]{1,0:T(1,128)}, u32[]{:S(2)}) copy-start(f32[1,512]{1,0:T(1,128)} %wi_ref.1) | copy-start | bytes 6148
  7.8 13.4 %copy-start.1 = (f32[2,3,8,8,128]{4,3,2,1,0:T(8,128)S(1)}, f32[2,3,8,8,128]{4,3,2,1,0:T(8,128)}, u32[]{:S(2)}) copy-start(f32[2,3,8,8,128]{4,3,2,1,0:T(8,128)} %param.22) | copy-start | bytes 589828
  7.8 13.4 %copy-start.3 = (f32[2,8,8,128]{3,2,1,0:T(8,128)S(1)}, f32[2,8,8,128]{3,2,1,0:T(8,128)}, u32[]{:S(2)}) copy-start(f32[2,8,8,128]{3,2,1,0:T(8,128)} %param.17) | copy-start | bytes 196612
  7.8 13.4 %copy-start.4 = (f32[3,8,8,128]{3,2,1,0:T(8,128)S(1)}, f32[3,8,8,128]{3,2,1,0:T(8,128)}, u32[]{:S(2)}) copy-start(f32[3,8,8,128]{3,2,1,0:T(8,128)} %param.20) | copy-start | bytes 294916
  7.8 13.4 %copy-start.6 = (f32[8,8,128]{2,1,0:T(8,128)S(1)}, f32[8,8,128]{2,1,0:T(8,128)}, u32[]{:S(2)}) copy-start(f32[8,8,128]{2,1,0:T(8,128)} %param.16) | copy-start | bytes 98308
  7.8 13.4 %copy-start.7 = (s32[8,8,128]{2,1,0:T(8,128)S(1)}, s32[8,8,128]{2,1,0:T(8,128)}, u32[]{:S(2)}) copy-start(s32[8,8,128]{2,1,0:T(8,128)} %param.21) | copy-start | bytes 98308
  7.8 13.4 %copy-start.13 = (s32[8,128]{1,0:T(8,128)S(1)}, s32[8,128]{1,0:T(8,128)}, u32[]{:S(2)}) copy-start(s32[8,128]{1,0:T(8,128)} %well_ref.3) | copy-start | bytes 12292
  7.9 13.4 %copy-start.14 = (f32[8,128]{1,0:T(8,128)S(1)}, f32[8,128]{1,0:T(8,128)}, u32[]{:S(2)}) copy-start(f32[8,128]{1,0:T(8,128)} %link_ref.3) | copy-start | bytes 12292
  7.9 31.5 %all-to-all-start = ((f32[32,32,128]{2,1,0:T(8,128)}), f32[32,32,128]{2,1,0:T(8,128)S(1)}, u32[]{:S(2)}, u32[]{:S(2)}) async-start(f32[32,32,128]{2,1,0:T(8,128)} %get-tuple-element.14), calls=%async_computation | async-start | bytes 1048576 | tf_op jit(solution)/shard_map/all_to_all | solution.py:383
  21.3 12.1 %copy-start.8 = (f32[3,8,8,128]{3,2,1,0:T(8,128)S(1)}, f32[3,8,8,128]{3,2,1,0:T(8,128)}, u32[]{:S(2)}) copy-start(f32[3,8,8,128]{3,2,1,0:T(8,128)} %param.18) | copy-start | bytes 294916
  21.3 12.1 %copy-start.11 = (f32[8,8,128]{2,1,0:T(8,128)S(1)}, f32[8,8,128]{2,1,0:T(8,128)}, u32[]{:S(2)}) copy-start(f32[8,8,128]{2,1,0:T(8,128)} %param.19) | copy-start | bytes 98308
  21.5 11.9 %collective-permute-start.1 = (f32[104,128]{1,0:T(8,128)S(1)}, f32[104,128]{1,0:T(8,128)S(1)}, u32[]{:S(2)}, u32[]{:S(2)}) collective-permute-start(f32[104,128]{1,0:T(8,128)S(1)} %get-tuple-element.17), channel_id=1, source_target_pairs={{0,16},{16,32},{32,48},{48,64},{64,80},{80,96},{96,112},{112,128},... | collective-permute-start | bytes 159752 | tf_op jit(solution)/shard_map/ppermute | solution.py:362
  25.2 8.2 %collective-permute-start = (f32[80,128]{1,0:T(8,128)S(1)}, f32[80,128]{1,0:T(8,128)S(1)}, u32[]{:S(2)}, u32[]{:S(2)}) collective-permute-start(f32[80,128]{1,0:T(8,128)S(1)} %get-tuple-element.16), channel_id=1, source_target_pairs={{16,0},{32,16},{48,32},{64,48},{80,64},{96,80},{112,96},{128,112},... | collective-permute-start | bytes 122888 | tf_op jit(solution)/shard_map/ppermute | solution.py:362
  26.5 4.3 %collective-permute-start.2 = (f32[8,128]{1,0:T(8,128)S(1)}, f32[8,128]{1,0:T(8,128)S(1)}, u32[]{:S(2)}, u32[]{:S(2)}) collective-permute-start(f32[8,128]{1,0:T(8,128)S(1)} %get-tuple-element.18.ylo_ref), channel_id=1, source_target_pairs={{1,0},{2,1},{3,2},{4,3},{5,4},{6,5},{7,6},{8,7},{9,8},{10,9},{11,1... | collective-permute-start | bytes 12296 | tf_op jit(solution)/shard_map/ppermute | solution.py:362
  28.5 4.9 %collective-permute-start.3 = (f32[8,128]{1,0:T(8,128)S(1)}, f32[8,128]{1,0:T(8,128)S(1)}, u32[]{:S(2)}, u32[]{:S(2)}) collective-permute-start(f32[8,128]{1,0:T(8,128)S(1)} %get-tuple-element.19.yhi_ref), channel_id=1, source_target_pairs={{0,1},{1,2},{2,3},{3,4},{4,5},{5,6},{6,7},{7,8},{8,9},{9,10},{10,1... | collective-permute-start | bytes 12296 | tf_op jit(solution)/shard_map/ppermute | solution.py:362
  33.4 5.9 %copy-start.10 = (f32[2,8,128]{2,1,0:T(8,128)S(1)}, f32[2,8,128]{2,1,0:T(8,128)}, u32[]{:S(2)}) copy-start(f32[2,8,128]{2,1,0:T(8,128)} %st_ref.3) | copy-start | bytes 24580
  33.4 5.9 %copy-start.19 = (f32[8,128]{1,0:T(8,128)S(1)}, f32[8,128]{1,0:T(8,128)}, u32[]{:S(2)}) copy-start(f32[8,128]{1,0:T(8,128)} %heel_ref.1) | copy-start | bytes 12292
  39.3 0.7 %copy-start.18 = (s32[1,512]{1,0:T(1,128)S(1)}, s32[1,512]{1,0:T(1,128)}, u32[]{:S(2)}) copy-start(s32[1,512]{1,0:T(1,128)} %ps_ref.3) | copy-start | bytes 6148
  39.3 0.7 %copy-start.16 = (s32[1,512]{1,0:T(1,128)S(1)}, s32[1,512]{1,0:T(1,128)}, u32[]{:S(2)}) copy-start(s32[1,512]{1,0:T(1,128)} %pc_ref.3) | copy-start | bytes 6148

commit v2 on v1

v2 whole, which is shorter than its diff:
```python
import jax
import jax.numpy as jnp
from jax import lax
from jax.experimental import pallas as pl
from jax.experimental.pallas import tpu as pltpu
from jax.sharding import PartitionSpec as P

COMPRESS = (0.05, 0.1, 0.6)
INV_VISCOSITY = (2.0, 0.5, 5.0)
GRAVITY_HEAD = (0.3, 0.25, 0.05)

NZ = 8
LANES = 128
CELL_ROWS = 64
SLOTS = 512
TILES = 32
PEER = 16
ROWS_A = 24
BLOCK = ROWS_A + 1
F32 = jnp.float32
BF16 = jnp.bfloat16
VMEM = pl.BlockSpec(memory_space=pltpu.VMEM)


def roll(x, shift, axis):
    return pltpu.roll(x, shift % x.shape[axis], axis)


def iota(shape, dim):
    return lax.broadcasted_iota(jnp.int32, shape, dim)


def split(x):
    hi = x.astype(BF16)
    lo = (x - hi.astype(F32)).astype(BF16)
    return hi, lo


def one_hot(mask):
    return jnp.where(mask, 1.0, 0.0).astype(BF16)


def properties(press, water, gas):
    oil = (1.0 - water[0] - gas[0], -water[1] - gas[1], -water[2] - gas[2])
    mobility, mass = [], []
    for phase, sat in enumerate((water, oil, gas)):
        c = COMPRESS[phase]
        base = jnp.exp(c * press[0])
        cb = c * base
        m0 = base * sat[0]
        cs = cb * sat[0]
        m1 = cs * press[1] + base * sat[1]
        m2 = cs * press[2] + base * sat[2]
        v = INV_VISCOSITY[phase]
        vs = v * sat[0]
        vm = v * m0
        mobility.append((m0 * vs, m1 * vs + vm * sat[1], m2 * vs + vm * sat[2]))
        mass.append((m0, m1, m2))
    return mobility, mass


def fluxes(mob_low, mob_up, press_low, press_up, trans, code, direction, heads):
    drop = [trans * (press_low[s] - press_up[s]) for s in range(3)]
    out = []
    for phase in range(3):
        bit = (code & (1 << (3 * direction + phase))) != 0
        up = [jnp.where(bit, mob_up[phase][s], mob_low[phase][s]) for s in range(3)]
        first = drop[0] if heads is None else drop[0] + trans * heads[phase]
        out.append(
            (
                up[0] * first,
                up[1] * first + up[0] * drop[1],
                up[2] * first + up[0] * drop[2],
            )
        )
    return out


def nine(p_ref, s_ref, ct_ref, at):
    return [
        p_ref[at, :], ct_ref[0, 0, at, :], ct_ref[1, 0, at, :],
        s_ref[0, at, :], ct_ref[0, 1, at, :], ct_ref[1, 1, at, :],
        s_ref[1, at, :], ct_ref[0, 2, at, :], ct_ref[1, 2, at, :],
    ]


def exchange(x):
    sub, group = iota((8, LANES), 0), iota((8, LANES), 1) >> 4
    for b in (1, 2, 4):
        s, g = (sub & b) != 0, (group & b) != 0
        down = roll(roll(x, -b, 0), PEER * b, 1)
        up = roll(roll(x, b, 0), -PEER * b, 1)
        x = jnp.where(s == g, x, jnp.where(g, down, up))
    return x


def slot_kernel(p_hbm, s_hbm, ct_hbm, sp_hbm, st_hbm, pc_hbm, ps_hbm, wi_hbm, cnt_hbm, pay_ref, slot_ref,
                p_ref, s_ref, ct_ref, sp_ref, st_ref, pc_ref, ps_ref, wi_ref, cnt_ref, sems):
    pairs = [
        (p_hbm, p_ref), (s_hbm, s_ref), (ct_hbm, ct_ref), (pc_hbm, pc_ref), (sp_hbm, sp_ref), (st_hbm, st_ref),
        (ps_hbm, ps_ref), (wi_hbm, wi_ref), (cnt_hbm, cnt_ref),
    ]
    copies = [pltpu.make_async_copy(src, dst, sems.at[n]) for n, (src, dst) in enumerate(pairs)]
    for copy in copies:
        copy.start()
    for copy in copies:
        copy.wait()
    seg = [sp_ref[...], st_ref[0], st_ref[1]]
    for k in range(TILES):
        for s in range(3):
            pay_ref[pl.ds(k * BLOCK + s * 8, 8), :] = seg[s]
    at = pl.ds(0, CELL_ROWS)
    hi, lo = split(jnp.concatenate(nine(p_ref, s_ref, ct_ref, at), 0))
    raw = jnp.concatenate([hi, lo], 1)
    cell = pc_ref[...]
    lane = cell & (LANES - 1)
    row = cell >> 7
    lane_hot = one_hot(iota((LANES, SLOTS), 0) == lane)
    picked = jnp.dot(raw, jnp.concatenate([lane_hot, lane_hot], 0), preferred_element_type=F32)
    row_mask = iota((CELL_ROWS, SLOTS), 0) == row
    val = [
        jnp.sum(jnp.where(row_mask, picked[q * CELL_ROWS:(q + 1) * CELL_ROWS], 0.0), axis=0, keepdims=True)
        for q in range(9)
    ]
    owner = iota((TILES, SLOTS), 1) >> 4
    tile_hot = one_hot(iota((TILES, SLOTS), 0) == owner)
    counts = jnp.broadcast_to(cnt_ref[...].astype(F32).astype(BF16), (8, TILES))
    live = jnp.dot(counts, tile_hot, preferred_element_type=F32)[0:1]
    rank = (iota((1, SLOTS), 1) & (PEER - 1)).astype(F32)
    weight = jnp.where(rank < live, wi_ref[...], 0.0)
    press = val[0:3]
    mobility, _ = properties(press, val[3:6], val[6:9])
    wl = [[weight * mobility[a][s] for s in range(3)] for a in range(3)]
    total = [wl[0][s] + wl[1][s] + wl[2][s] for s in range(3)]
    carry = [
        total[0] * press[0],
        total[1] * press[0] + total[0] * press[1],
        total[2] * press[0] + total[0] * press[2],
    ]
    number = ps_ref[...].astype(F32)
    slot_ref[...] = jnp.concatenate(
        press + [wl[a][s] for s in range(3) for a in range(3)]
        + [cell.astype(F32), number, jnp.zeros((2, SLOTS), F32)], 0
    )
    sent = jnp.concatenate([number] + carry + total + [jnp.zeros((1, SLOTS), F32)], 0)
    for w in range(4):
        rows = exchange(sent[:, w * LANES:(w + 1) * LANES])
        for k in range(8):
            pay_ref[pl.ds((w * 8 + k) * BLOCK + ROWS_A, 1), :] = rows[k:k + 1]


def pack_kernel(p_ref, s_ref, ct_ref, t_ref, code_ref, sp_ref, st_ref, well_ref, link_ref, heel_ref,
                xlo_ref, xhi_ref, ylo_ref, yhi_ref, seg_ref):
    first, last = pl.ds(0, NZ, stride=8), pl.ds(7, NZ, stride=8)
    for q, v in enumerate(nine(p_ref, s_ref, ct_ref, first)):
        xlo_ref[q * 8:(q + 1) * 8, :] = v
    for q, v in enumerate(nine(p_ref, s_ref, ct_ref, last)):
        xhi_ref[q * 8:(q + 1) * 8, :] = v
    xhi_ref[72:80, :] = t_ref[0, last, :]
    xhi_ref[80:88, :] = code_ref[last, :].astype(F32)
    lane = iota((8, LANES), 1)
    seg = [well_ref[...].astype(F32), link_ref[...], sp_ref[...], st_ref[0], st_ref[1], heel_ref[...]]
    for n, v in enumerate(seg):
        seg_ref[n * 8:(n + 1) * 8, :] = v
    left, right = seg[0], seg[0]
    for n in range(1, 5):
        left = jnp.where(lane == n, roll(seg[n], n, 1), left)
        right = jnp.where(lane == LANES - 1 - n, roll(seg[n], -n, 1), right)
    xlo_ref[72:80, :] = left
    xhi_ref[88:96, :] = right
    low = jnp.zeros((8, LANES), F32)
    high = jnp.zeros((8, LANES), F32)
    for z in range(NZ):
        at = pl.ds(z * 8, 8)
        for q, v in enumerate(nine(p_ref, s_ref, ct_ref, at)):
            c = q * 8 + z
            low = jnp.where(lane == c, roll(v, c, 1), low)
            high = jnp.where(lane == c, roll(v, c + 1, 1), high)
        high = jnp.where(lane == 72 + z, roll(t_ref[1, at, :], 73 + z, 1), high)
        high = jnp.where(lane == 80 + z, roll(code_ref[at, :].astype(F32), 81 + z, 1), high)
    ylo_ref[...] = low
    yhi_ref[...] = high


def stencil_kernel(p_ref, s_ref, ct_ref, om_ref, pv_ref, t_ref, code_ref, bal_ref):
    lane = iota((8, LANES), 1)
    sub = iota((8, LANES), 0)
    raw = nine(p_ref, s_ref, ct_ref, pl.ds(0, 8))
    mob, mass = properties(raw[0:3], raw[3:6], raw[6:9])
    press = raw[0:3]
    above = None
    for z in range(NZ):
        at = pl.ds(z * 8, 8)
        code = code_ref[at, :]
        volume = pv_ref[at, :]
        bal = [[volume * mass[a][s] for s in range(3)] for a in range(3)]
        for a in range(3):
            bal[a][0] = bal[a][0] - om_ref[a, at, :]
        for direction, axis, last in ((0, 0, sub == 7), (1, 1, lane == LANES - 1)):
            trans = jnp.where(last, 0.0, t_ref[direction, at, :])
            up_mob = [[roll(mob[a][s], -1, axis) for s in range(3)] for a in range(3)]
            up_press = [roll(press[s], -1, axis) for s in range(3)]
            flux = fluxes(mob, up_mob, press, up_press, trans, code, direction, None)
            for a in range(3):
                for s in range(3):
                    bal[a][s] = bal[a][s] + (flux[a][s] - roll(flux[a][s], 1, axis))
        if above is not None:
            for a in range(3):
                for s in range(3):
                    bal[a][s] = bal[a][s] - above[a][s]
        if z < NZ - 1:
            raw = nine(p_ref, s_ref, ct_ref, pl.ds(z * 8 + 8, 8))
            mob_next, mass = properties(raw[0:3], raw[3:6], raw[6:9])
            above = fluxes(mob, mob_next, press, raw[0:3], t_ref[2, at, :], code, 2, GRAVITY_HEAD)
            for a in range(3):
                for s in range(3):
                    bal[a][s] = bal[a][s] + above[a][s]
            mob, press = mob_next, raw[0:3]
        for a in range(3):
            for s in range(3):
                bal_ref[s * 3 + a, at, :] = bal[a][s]


def face(low, up, trans, code, direction):
    return fluxes(
        properties(low[0:3], low[3:6], low[6:9])[0], properties(up[0:3], up[3:6], up[6:9])[0],
        low[0:3], up[0:3], trans, code, direction, None,
    )


def join_kernel(got_ref, slot_ref, bal_ref, seg_ref, xlo_ref, xhi_ref, ylo_ref, yhi_ref,
                exlo_ref, wxhi_ref, nylo_ref, syhi_ref, res_ref, prod_ref, segout_ref):
    top_x = lax.axis_index("xt") == TILES - 1
    top_y = lax.axis_index("yt") == lax.axis_size("yt") - 1
    lane = iota((8, LANES), 1)
    group = iota((1, LANES), 1) >> 4

    seg_number = slot_ref[13:14, :].astype(jnp.int32)
    seg_lane = seg_number & (LANES - 1)
    seg_row = seg_number >> 7
    rates = [[] for _ in range(9)]
    for w in range(4):
        cols = slice(w * LANES, (w + 1) * LANES)
        hot = one_hot(iota((LANES, LANES), 0) == seg_lane[:, cols])
        blocks = [got_ref[pl.ds((w * 8 + k) * BLOCK, ROWS_A), :] for k in range(8)]
        hi, lo = split(jnp.concatenate(blocks, 0))
        picked = jnp.dot(
            jnp.concatenate([hi, lo], 1), jnp.concatenate([hot, hot], 0), preferred_element_type=F32
        )
        mine = picked[0:ROWS_A]
        for k in range(1, 8):
            mine = jnp.where(group == k, picked[k * ROWS_A:(k + 1) * ROWS_A], mine)
        row_mask = iota((8, LANES), 0) == seg_row[:, cols]
        at_seg = [
            jnp.sum(jnp.where(row_mask, mine[s * 8:(s + 1) * 8], 0.0), axis=0, keepdims=True) for s in range(3)
        ]
        drop = [slot_ref[s:s + 1, cols] - at_seg[s] for s in range(3)]
        base = [slot_ref[3 + a:4 + a, cols] for a in range(3)]
        for a in range(3):
            rates[a].append(base[a] * drop[0])
            for s in (1, 2):
                r = 3 + s * 3 + a
                rates[s * 3 + a].append(slot_ref[r:r + 1, cols] * drop[0] + base[a] * drop[s])

    cell = slot_ref[12:13, :].astype(jnp.int32)
    lane_hot = one_hot(iota((LANES, SLOTS), 0) == (cell & (LANES - 1)))
    row_hot = one_hot(iota((CELL_ROWS, SLOTS), 0) == (cell >> 7))
    parts = [split(jnp.concatenate(r, 1)) for r in rates]
    left = jnp.concatenate(
        [jnp.concatenate([row_hot * hi, row_hot * lo], 1) for hi, lo in parts], 0
    )
    added = lax.dot_general(
        left, jnp.concatenate([lane_hot, lane_hot], 1), (((1,), (1,)), ((), ())), preferred_element_type=F32
    )

    half = lane < 64
    own_lo, own_hi, north, south = ylo_ref[...], yhi_ref[...], nylo_ref[...], syhi_ref[...]
    low = [jnp.where(half, roll(own_hi, -8 * q, 1), roll(south, 64 - 8 * q, 1)) for q in range(11)]
    up = [jnp.where(half, roll(north, -8 * q, 1), roll(own_lo, 64 - 8 * q, 1)) for q in range(9)]
    trans = jnp.where(jnp.logical_and(half, top_y), 0.0, low[9])
    rim = face(low[0:9], up, trans, low[10].astype(jnp.int32), 1)
    even = (lane & 1) == 0
    edge = jnp.logical_or(lane == 0, lane == LANES - 1)

    def planes(ref, count):
        return [ref[q * 8:(q + 1) * 8, :] for q in range(count)]

    own, near = planes(xhi_ref, 11), planes(wxhi_ref, 11)
    east = face(own[0:9], planes(exlo_ref, 9), jnp.where(top_x, 0.0, own[9]), own[10].astype(jnp.int32), 0)
    west = face(near[0:9], planes(xlo_ref, 9), near[9], near[10].astype(jnp.int32), 0)
    first, last = pl.ds(0, NZ, stride=8), pl.ds(7, NZ, stride=8)

    for s in range(3):
        for a in range(3):
            n = s * 3 + a
            flux = rim[a][s]
            moved = roll(flux, 65, 1)
            by_parity = (jnp.where(even, flux, -moved), jnp.where(even, -moved, flux))
            out = res_ref.at[a] if s == 0 else prod_ref.at[s - 1, a]
            for z in range(NZ):
                at = pl.ds(z * 8, 8)
                rim_z = jnp.where(edge, roll(by_parity[z % 2], LANES - 1 - z, 1), 0.0)
                out[at, :] = bal_ref[n, at, :] + added[n * CELL_ROWS + z * 8:n * CELL_ROWS + z * 8 + 8] + rim_z
            out[last, :] = out[last, :] + east[a][s]
            out[first, :] = out[first, :] - west[a][s]

    told = jnp.concatenate(
        [exchange(got_ref[pl.ds(w * 8 * BLOCK + ROWS_A, 8, stride=BLOCK), :]) for w in range(4)], 1
    )
    number = told[0:1].astype(jnp.int32)
    hot = one_hot(iota((LANES, SLOTS), 0) == (number & (LANES - 1)))
    row_mask = iota((8, SLOTS), 0) == (number >> 7)
    hi, lo = split(jnp.concatenate([jnp.where(row_mask, told[q:q + 1], 0.0) for q in range(1, 7)], 0))
    sums = lax.dot_general(
        jnp.concatenate([hi, lo], 1), jnp.concatenate([hot, hot], 1), (((1,), (1,)), ((), ())),
        preferred_element_type=F32,
    )
    c = [sums[s * 8:(s + 1) * 8] for s in range(3)]
    a = [sums[24 + s * 8:32 + s * 8] for s in range(3)]
    well, link, *seg = planes(seg_ref, 5)
    heel = seg_ref[40:48, :]
    inflow = [
        c[0] - seg[0] * a[0],
        c[1] - seg[0] * a[1] - seg[1] * a[0],
        c[2] - seg[0] * a[2] - seg[2] * a[0],
    ]

    after, before = exlo_ref[72:80, :], wxhi_ref[88:96, :]
    lane0 = lane == 0
    next_well = roll(jnp.where(lane0, after, well), -1, 1)
    linked = jnp.logical_and(next_well == well, jnp.logical_not(jnp.logical_and(top_x, lane == LANES - 1)))
    joined = roll(before, 1, 1) == well
    link_west = roll(before, 2, 1)
    for s in range(3):
        next_press = roll(jnp.where(lane0, roll(after, -2 - s, 1), seg[s]), -1, 1)
        end = heel if s == 0 else jnp.zeros((8, LANES), F32)
        flow = link * (seg[s] - jnp.where(linked, next_press, end))
        carried = jnp.where(linked, flow, 0.0)
        entering = jnp.where(joined, link_west * (roll(before, 3 + s, 1) - seg[s]), 0.0)
        segout_ref[s] = inflow[s] - flow + jnp.where(lane0, entering, roll(carried, 1, 1))


def call(kernel, out_shapes, *args, in_spec=VMEM, scratch=()):
    return pl.pallas_call(
        kernel,
        out_shape=[jax.ShapeDtypeStruct(s, F32) for s in out_shapes],
        in_specs=[in_spec] * len(args),
        out_specs=[VMEM] * len(out_shapes),
        scratch_shapes=scratch,
        compiler_params=pltpu.CompilerParams(vmem_limit_bytes=16 * 2**20),
    )(*args)


def call_loading(kernel, out_shapes, *args):
    scratch = [pltpu.VMEM(a.shape, a.dtype) for a in args] + [pltpu.SemaphoreType.DMA((len(args),))]
    args = [pltpu.with_memory_space_constraint(a, pltpu.HBM) for a in args]
    return call(kernel, out_shapes, *args, in_spec=pl.BlockSpec(memory_space=pltpu.HBM), scratch=scratch)


def shift(array, axis, by):
    length = lax.axis_size(axis)
    return lax.ppermute(array, axis, [(i, i + by) for i in range(length) if 0 <= i + by < length])


def body(
    pressure, saturation, old_mass, pore_volume, transmissibility, upwind_code, cell_tangent, segment_pressure,
    segment_tangent, segment_well, link_factor, heel_pressure, perforation_cell, perforation_segment, well_index,
    perforation_count,
):
    p = pressure.reshape(CELL_ROWS, LANES)
    sat = saturation.reshape(2, CELL_ROWS, LANES)
    om = old_mass.reshape(3, CELL_ROWS, LANES)
    pv = pore_volume.reshape(CELL_ROWS, LANES)
    tr = transmissibility.reshape(3, CELL_ROWS, LANES)
    code = upwind_code.reshape(CELL_ROWS, LANES)
    ct = cell_tangent.reshape(2, 3, CELL_ROWS, LANES)

    pay, slots = call_loading(
        slot_kernel, [(TILES * BLOCK, LANES), (16, SLOTS)],
        p, sat, ct, segment_pressure, segment_tangent, perforation_cell, perforation_segment, well_index,
        perforation_count,
    )
    got = lax.all_to_all(pay.reshape(TILES, 1, BLOCK * LANES), "xt", 0, 0, tiled=True)
    got = got.reshape(TILES * BLOCK, LANES)
    xlo, xhi, ylo, yhi, seg = call(
        pack_kernel, [(80, LANES), (96, LANES), (8, LANES), (8, LANES), (48, LANES)],
        p, sat, ct, tr, code, segment_pressure, segment_tangent, segment_well, link_factor, heel_pressure,
    )
    west_xhi = shift(xhi, "xt", 1)
    east_xlo = shift(xlo, "xt", -1)
    north_ylo = shift(ylo, "yt", -1)
    south_yhi = shift(yhi, "yt", 1)
    (bal,) = call(stencil_kernel, [(9, CELL_ROWS, LANES)], p, sat, ct, om, pv, tr, code)
    res, prod, seg = call(
        join_kernel, [(3, CELL_ROWS, LANES), (2, 3, CELL_ROWS, LANES), (3, 8, LANES)],
        got, slots, bal, seg, xlo, xhi, ylo, yhi, east_xlo, west_xhi, north_ylo, south_yhi,
    )
    return (res.reshape(old_mass.shape), prod.reshape(cell_tangent.shape), seg)


def solution(mesh):
    cell, seg = P(None, "xt", "yt"), P("yt", "xt")
    cell2, cell3, seg2 = P(None, None, "xt", "yt"), P(None, None, None, "xt", "yt"), P(None, "yt", "xt")
    in_specs = (
        cell, cell2, cell2, cell, cell2, cell, cell3, seg, seg2, seg, seg, seg, seg, seg, seg, seg,
    )
    return jax.shard_map(body, mesh=mesh, in_specs=in_specs, out_specs=(cell2, cell3, seg2), check_vma=False)
```

time: 43.1 us -> 34.7 us (0.81)
  local copies, waits for them, and re-layouts: 6.68 us -> 0.08 us
  Pallas kernels: 5.28 us -> 4.49 us
  waiting for transfers between devices: 7 us -> 6.29 us
    unnamed x44 -> x24, local copies, waits for them, and re-layouts: 6.68 us -> 0.08 us
    pallas_call x4, Pallas kernels: 5.28 us -> 4.49 us  [call(): pl.pallas_call(kernel, out_shape=[jax.ShapeDtypeStruct(s, F32) for s in o...]
  transfers between devices with their start and end apart: 5 -> 5, of which waited for: 2 -> 2; matrix products, arithmetic and copies ran while one was open for 0% -> 0% of each run, Pallas kernels for 4% -> 2%
where the time goes in v2:
time: 34.7 us; the launch traced here: 34.4 us
  starting transfers between devices  22.6 us (65%)
  waiting for transfers between devices  6.29 us (18%)
  Pallas kernels  4.49 us (13%)
  between operations  0.89 us (3%)
    all_to_all x1, starting transfers between devices, body(): lax.all_to_all(pay.reshape(TILES, 1, BLOCK * LANES), 'xt', 0, 0, tiled=True)  13.3 us
    ppermute x4, starting transfers between devices, shift(): lax.ppermute(array, axis, [(i, i + by) for i in range(length) if 0 <= i +...  9.31 us
    pallas_call x4, Pallas kernels, call(): pl.pallas_call(kernel, out_shape=[jax.ShapeDtypeStruct(s, F32) for s in o...  4.49 us
    all_to_all x1, waiting for transfers between devices, body(): lax.all_to_all(pay.reshape(TILES, 1, BLOCK * LANES), 'xt', 0, 0, tiled=True)  4.16 us
    ppermute x4, waiting for transfers between devices, shift(): lax.ppermute(array, axis, [(i, i + by) for i in range(length) if 0 <= i +...  2.13 us
  transfers between devices with their start and end apart: 5, of which 2 were waited for; matrix products, arithmetic and copies ran while one was open for 0% of the time, Pallas kernels for 2%

profile of v2, /device:TPU:56, one launch (start us, length us, event | category | flops | bytes accessed | tf_op | source)
XLA Modules:
  0.0 34.4 jit_solution(17677864514538889643)
XLA Ops:
  0.6 2.4 %shard_map.175 = (f32[800,128]{1,0:T(8,128)}, f32[16,512]{1,0:T(8,128)S(1)}) custom-call(f32[64,128]{1,0:T(8,128)} %bitcast.20, f32[2,64,128]{2,1,0:T(8,128)} %bitcast.15, f32[2,3,64,128]{3,2,1,0:T(8,128)} %bitcast.11, f32[8,128]{1,0:T(8,128)} %sp_ref.1, f32[2,8,128]{2,1,0:T(8,128)} %st_ref.1, s32[1,512]{1,0:T(1,128)} %pc_hbm.1, s32[1,512]{1,0:T(1,128)} %ps_hbm.1, ...), custom_call_target="tpu_custom_call" | custom-call | tf_op jit(solution)/shard_map/pallas_call | solution.py:344
  3.1 0.0 copy-start
  3.1 0.0 copy-start.1
  3.1 0.0 copy-start.2
  3.1 0.0 copy-start.3
  3.1 0.0 copy-start.4
  3.1 0.0 copy-start.6
  3.1 0.0 copy-start.8
  3.2 0.0 copy-start.9
  3.2 0.0 copy-start.10
  3.2 0.0 copy-start.11
  3.2 13.3 %all-to-all-start = ((f32[32,1,3200]{2,1,0:T(1,128)}), f32[32,1,3200]{2,1,0:T(1,128)S(1)}, u32[]{:S(2)}, u32[]{:S(2)}) async-start(f32[32,1,3200]{2,1,0:T(1,128)} %bitcast.3), calls=%async_computation | async-start | bytes 819200 | tf_op jit(solution)/shard_map/all_to_all | solution.py:383
  16.5 0.0 copy-done
  16.5 0.0 copy-done.1
  16.5 0.0 copy-done.2
  16.5 0.0 copy-done.3
  16.5 0.0 copy-done.4
  16.6 0.0 copy-done.6
  16.6 0.0 copy-done.8
  16.6 0.0 copy-done.9
  16.6 0.0 copy-done.10
  16.6 0.0 copy-done.11
  16.6 0.0 copy-start.5
  16.6 0.0 copy-start.7
  16.6 0.2 shard_map.177
  16.9 3.7 %collective-permute-start.1 = (f32[96,128]{1,0:T(8,128)S(1)}, f32[96,128]{1,0:T(8,128)S(1)}, u32[]{:S(2)}, u32[]{:S(2)}) collective-permute-start(f32[96,128]{1,0:T(8,128)S(1)} %get-tuple-element.17.xhi_ref), channel_id=1, source_target_pairs={{0,16},{16,32},{32,48},{48,64},{64,80},{80,96},{96,112},{112,128},... | collective-permute-start | bytes 147464 | tf_op jit(solution)/shard_map/ppermute | solution.py:362
  20.6 1.3 %collective-permute-start = (f32[80,128]{1,0:T(8,128)S(1)}, f32[80,128]{1,0:T(8,128)S(1)}, u32[]{:S(2)}, u32[]{:S(2)}) collective-permute-start(f32[80,128]{1,0:T(8,128)S(1)} %get-tuple-element.16.xlo_ref), channel_id=1, source_target_pairs={{16,0},{32,16},{48,32},{64,48},{80,64},{96,80},{112,96},{128,112},... | collective-permute-start | bytes 122888 | tf_op jit(solution)/shard_map/ppermute | solution.py:362
  21.9 1.9 %collective-permute-start.2 = (f32[8,128]{1,0:T(8,128)S(1)}, f32[8,128]{1,0:T(8,128)S(1)}, u32[]{:S(2)}, u32[]{:S(2)}) collective-permute-start(f32[8,128]{1,0:T(8,128)S(1)} %get-tuple-element.18.ylo_ref), channel_id=1, source_target_pairs={{1,0},{2,1},{3,2},{4,3},{5,4},{6,5},{7,6},{8,7},{9,8},{10,9},{11,1... | collective-permute-start | bytes 12296 | tf_op jit(solution)/shard_map/ppermute | solution.py:362
  23.8 2.4 %collective-permute-start.3 = (f32[8,128]{1,0:T(8,128)S(1)}, f32[8,128]{1,0:T(8,128)S(1)}, u32[]{:S(2)}, u32[]{:S(2)}) collective-permute-start(f32[8,128]{1,0:T(8,128)S(1)} %get-tuple-element.19.yhi_ref), channel_id=1, source_target_pairs={{0,1},{1,2},{2,3},{3,4},{4,5},{5,6},{6,7},{7,8},{8,9},{9,10},{10,1... | collective-permute-start | bytes 12296 | tf_op jit(solution)/shard_map/ppermute | solution.py:362
  26.2 0.0 copy-done.5
  26.2 0.0 copy-done.7
  26.2 0.4 %shard_map.176.bal_ref = f32[9,64,128]{2,1,0:T(8,128)S(1)} custom-call(f32[64,128]{1,0:T(8,128)S(1)} %bitcast.22, f32[2,64,128]{2,1,0:T(8,128)S(1)} %bitcast.17, f32[2,3,64,128]{3,2,1,0:T(8,128)S(1)} %bitcast.13, f32[3,64,128]{2,1,0:T(8,128)S(1)} %bitcast.25, f32[64,128]{1,0:T(8,128)S(1)} %bitcast.26, f32[3,64,128]{2,1,0:T(8,128)S(1)} %bitcast.19, ...), custom_call_target="tpu_custom_call" | custom-call | tf_op jit(solution)/shard_map/pallas_call | solution.py:344
  26.6 0.0 collective-permute-done.2.nylo_ref
  26.6 2.1 %collective-permute-done.3.syhi_ref = f32[8,128]{1,0:T(8,128)S(1)} collective-permute-done((f32[8,128]{1,0:T(8,128)S(1)}, f32[8,128]{1,0:T(8,128)S(1)}, u32[]{:S(2)}, u32[]{:S(2)}) %collective-permute-start.3) | collective-permute-done | bytes 4128 | tf_op jit(solution)/shard_map/ppermute | solution.py:362
  28.7 0.0 collective-permute-done.exlo_ref
  28.7 0.0 collective-permute-done.1.wxhi_ref
  28.7 4.2 %all-to-all-done = f32[32,1,3200]{2,1,0:T(1,128)S(1)} async-done(((f32[32,1,3200]{2,1,0:T(1,128)}), f32[32,1,3200]{2,1,0:T(1,128)S(1)}, u32[]{:S(2)}, u32[]{:S(2)}) %all-to-all-start) | async-done | bytes 409632 | tf_op jit(solution)/shard_map/all_to_all | solution.py:383
  32.9 1.5 %shard_map.178 = (f32[3,64,128]{2,1,0:T(8,128)}, f32[2,3,64,128]{3,2,1,0:T(8,128)}, f32[3,8,128]{2,1,0:T(8,128)}) custom-call(f32[800,128]{1,0:T(8,128)S(1)} %bitcast.14, f32[16,512]{1,0:T(8,128)S(1)} %get-tuple-element.14.slot_ref, f32[9,64,128]{2,1,0:T(8,128)S(1)} %shard_map.176.bal_ref, f32[48,128]{1,0:T(8,128)S(1)} %get-tuple-element.15.seg_ref, ...), custom_call_target="tpu_custom_call" | custom-call | tf_op jit(solution)/shard_map/pallas_call | solution.py:344
Async XLA Ops:
  3.1 13.4 %copy-start = (f32[2,3,8,8,128]{4,3,2,1,0:T(8,128)S(1)}, f32[2,3,8,8,128]{4,3,2,1,0:T(8,128)}, u32[]{:S(2)}) copy-start(f32[2,3,8,8,128]{4,3,2,1,0:T(8,128)} %param.22) | copy-start | bytes 589828
  3.1 13.4 %copy-start.1 = (f32[2,8,8,128]{3,2,1,0:T(8,128)S(1)}, f32[2,8,8,128]{3,2,1,0:T(8,128)}, u32[]{:S(2)}) copy-start(f32[2,8,8,128]{3,2,1,0:T(8,128)} %param.17) | copy-start | bytes 196612
  3.1 13.4 %copy-start.2 = (f32[3,8,8,128]{3,2,1,0:T(8,128)S(1)}, f32[3,8,8,128]{3,2,1,0:T(8,128)}, u32[]{:S(2)}) copy-start(f32[3,8,8,128]{3,2,1,0:T(8,128)} %param.20) | copy-start | bytes 294916
  3.1 13.4 %copy-start.3 = (f32[8,8,128]{2,1,0:T(8,128)S(1)}, f32[8,8,128]{2,1,0:T(8,128)}, u32[]{:S(2)}) copy-start(f32[8,8,128]{2,1,0:T(8,128)} %param.16) | copy-start | bytes 98308
  3.1 13.4 %copy-start.4 = (s32[8,8,128]{2,1,0:T(8,128)S(1)}, s32[8,8,128]{2,1,0:T(8,128)}, u32[]{:S(2)}) copy-start(s32[8,8,128]{2,1,0:T(8,128)} %param.21) | copy-start | bytes 98308
  3.1 13.4 %copy-start.6 = (f32[2,8,128]{2,1,0:T(8,128)S(1)}, f32[2,8,128]{2,1,0:T(8,128)}, u32[]{:S(2)}) copy-start(f32[2,8,128]{2,1,0:T(8,128)} %st_ref.1) | copy-start | bytes 24580
  3.1 13.4 %copy-start.8 = (f32[8,128]{1,0:T(8,128)S(1)}, f32[8,128]{1,0:T(8,128)}, u32[]{:S(2)}) copy-start(f32[8,128]{1,0:T(8,128)} %sp_ref.1) | copy-start | bytes 12292
  3.2 13.4 %copy-start.9 = (s32[8,128]{1,0:T(8,128)S(1)}, s32[8,128]{1,0:T(8,128)}, u32[]{:S(2)}) copy-start(s32[8,128]{1,0:T(8,128)} %well_ref.1) | copy-start | bytes 12292
  3.2 13.4 %copy-start.10 = (f32[8,128]{1,0:T(8,128)S(1)}, f32[8,128]{1,0:T(8,128)}, u32[]{:S(2)}) copy-start(f32[8,128]{1,0:T(8,128)} %link_ref.1) | copy-start | bytes 12292
  3.2 13.4 %copy-start.11 = (f32[8,128]{1,0:T(8,128)S(1)}, f32[8,128]{1,0:T(8,128)}, u32[]{:S(2)}) copy-start(f32[8,128]{1,0:T(8,128)} %heel_ref.1) | copy-start | bytes 12292
  3.2 29.7 %all-to-all-start = ((f32[32,1,3200]{2,1,0:T(1,128)}), f32[32,1,3200]{2,1,0:T(1,128)S(1)}, u32[]{:S(2)}, u32[]{:S(2)}) async-start(f32[32,1,3200]{2,1,0:T(1,128)} %bitcast.3), calls=%async_computation | async-start | bytes 819200 | tf_op jit(solution)/shard_map/all_to_all | solution.py:383
  16.6 9.6 %copy-start.5 = (f32[3,8,8,128]{3,2,1,0:T(8,128)S(1)}, f32[3,8,8,128]{3,2,1,0:T(8,128)}, u32[]{:S(2)}) copy-start(f32[3,8,8,128]{3,2,1,0:T(8,128)} %param.18) | copy-start | bytes 294916
  16.6 9.6 %copy-start.7 = (f32[8,8,128]{2,1,0:T(8,128)S(1)}, f32[8,8,128]{2,1,0:T(8,128)}, u32[]{:S(2)}) copy-start(f32[8,8,128]{2,1,0:T(8,128)} %param.19) | copy-start | bytes 98308
  16.9 11.9 %collective-permute-start.1 = (f32[96,128]{1,0:T(8,128)S(1)}, f32[96,128]{1,0:T(8,128)S(1)}, u32[]{:S(2)}, u32[]{:S(2)}) collective-permute-start(f32[96,128]{1,0:T(8,128)S(1)} %get-tuple-element.17.xhi_ref), channel_id=1, source_target_pairs={{0,16},{16,32},{32,48},{48,64},{64,80},{80,96},{96,112},{112,128},... | collective-permute-start | bytes 147464 | tf_op jit(solution)/shard_map/ppermute | solution.py:362
  20.6 8.2 %collective-permute-start = (f32[80,128]{1,0:T(8,128)S(1)}, f32[80,128]{1,0:T(8,128)S(1)}, u32[]{:S(2)}, u32[]{:S(2)}) collective-permute-start(f32[80,128]{1,0:T(8,128)S(1)} %get-tuple-element.16.xlo_ref), channel_id=1, source_target_pairs={{16,0},{32,16},{48,32},{64,48},{80,64},{96,80},{112,96},{128,112},... | collective-permute-start | bytes 122888 | tf_op jit(solution)/shard_map/ppermute | solution.py:362
  21.9 4.7 %collective-permute-start.2 = (f32[8,128]{1,0:T(8,128)S(1)}, f32[8,128]{1,0:T(8,128)S(1)}, u32[]{:S(2)}, u32[]{:S(2)}) collective-permute-start(f32[8,128]{1,0:T(8,128)S(1)} %get-tuple-element.18.ylo_ref), channel_id=1, source_target_pairs={{1,0},{2,1},{3,2},{4,3},{5,4},{6,5},{7,6},{8,7},{9,8},{10,9},{11,1... | collective-permute-start | bytes 12296 | tf_op jit(solution)/shard_map/ppermute | solution.py:362
  23.8 4.9 %collective-permute-start.3 = (f32[8,128]{1,0:T(8,128)S(1)}, f32[8,128]{1,0:T(8,128)S(1)}, u32[]{:S(2)}, u32[]{:S(2)}) collective-permute-start(f32[8,128]{1,0:T(8,128)S(1)} %get-tuple-element.19.yhi_ref), channel_id=1, source_target_pairs={{0,1},{1,2},{2,3},{3,4},{4,5},{5,6},{6,7},{7,8},{8,9},{9,10},{10,1... | collective-permute-start | bytes 12296 | tf_op jit(solution)/shard_map/ppermute | solution.py:362

commit v3 on v2

--- a/solution.py
+++ b/solution.py
@@ -17,6 +17,8 @@
 PEER = 16
 ROWS_A = 24
 BLOCK = ROWS_A + 1
+WIDE = 256
+WIDE_ROWS = 32
 F32 = jnp.float32
 BF16 = jnp.bfloat16
 VMEM = pl.BlockSpec(memory_space=pltpu.VMEM)
@@ -94,40 +96,46 @@
     return x
 
 
+def planes(ref, count):
+    return [ref[q * 8:(q + 1) * 8, :] for q in range(count)]
+
+
 def slot_kernel(p_hbm, s_hbm, ct_hbm, sp_hbm, st_hbm, pc_hbm, ps_hbm, wi_hbm, cnt_hbm, pay_ref, slot_ref,
                 p_ref, s_ref, ct_ref, sp_ref, st_ref, pc_ref, ps_ref, wi_ref, cnt_ref, sems):
     pairs = [
-        (p_hbm, p_ref), (s_hbm, s_ref), (ct_hbm, ct_ref), (pc_hbm, pc_ref), (sp_hbm, sp_ref), (st_hbm, st_ref),
-        (ps_hbm, ps_ref), (wi_hbm, wi_ref), (cnt_hbm, cnt_ref),
+        (pc_hbm, pc_ref), (sp_hbm, sp_ref), (st_hbm, st_ref), (cnt_hbm, cnt_ref), (wi_hbm, wi_ref), (ps_hbm, ps_ref),
+        (p_hbm, p_ref), (s_hbm, s_ref), (ct_hbm, ct_ref),
     ]
     copies = [pltpu.make_async_copy(src, dst, sems.at[n]) for n, (src, dst) in enumerate(pairs)]
     for copy in copies:
         copy.start()
-    for copy in copies:
+    owner = iota((TILES, SLOTS), 1) >> 4
+    tile_hot = one_hot(iota((TILES, SLOTS), 0) == owner)
+    copies[0].wait()
+    cell = pc_ref[...]
+    lane_hot = one_hot(iota((LANES, SLOTS), 0) == (cell & (LANES - 1)))
+    lane_hot = jnp.concatenate([lane_hot, lane_hot], 0)
+    row_mask = iota((CELL_ROWS, SLOTS), 0) == (cell >> 7)
+    for copy in copies[1:6]:
         copy.wait()
     seg = [sp_ref[...], st_ref[0], st_ref[1]]
     for k in range(TILES):
         for s in range(3):
             pay_ref[pl.ds(k * BLOCK + s * 8, 8), :] = seg[s]
+    counts = jnp.broadcast_to(cnt_ref[...].astype(F32).astype(BF16), (8, TILES))
+    live = jnp.dot(counts, tile_hot, preferred_element_type=F32)[0:1]
+    rank = (iota((1, SLOTS), 1) & (PEER - 1)).astype(F32)
+    weight = jnp.where(rank < live, wi_ref[...], 0.0)
+    number = ps_ref[...].astype(F32)
+    for copy in copies[6:]:
+        copy.wait()
     at = pl.ds(0, CELL_ROWS)
     hi, lo = split(jnp.concatenate(nine(p_ref, s_ref, ct_ref, at), 0))
-    raw = jnp.concatenate([hi, lo], 1)
-    cell = pc_ref[...]
-    lane = cell & (LANES - 1)
-    row = cell >> 7
-    lane_hot = one_hot(iota((LANES, SLOTS), 0) == lane)
-    picked = jnp.dot(raw, jnp.concatenate([lane_hot, lane_hot], 0), preferred_element_type=F32)
-    row_mask = iota((CELL_ROWS, SLOTS), 0) == row
+    picked = jnp.dot(jnp.concatenate([hi, lo], 1), lane_hot, preferred_element_type=F32)
     val = [
         jnp.sum(jnp.where(row_mask, picked[q * CELL_ROWS:(q + 1) * CELL_ROWS], 0.0), axis=0, keepdims=True)
         for q in range(9)
     ]
-    owner = iota((TILES, SLOTS), 1) >> 4
-    tile_hot = one_hot(iota((TILES, SLOTS), 0) == owner)
-    counts = jnp.broadcast_to(cnt_ref[...].astype(F32).astype(BF16), (8, TILES))
-    live = jnp.dot(counts, tile_hot, preferred_element_type=F32)[0:1]
-    rank = (iota((1, SLOTS), 1) & (PEER - 1)).astype(F32)
-    weight = jnp.where(rank < live, wi_ref[...], 0.0)
     press = val[0:3]
     mobility, _ = properties(press, val[3:6], val[6:9])
     wl = [[weight * mobility[a][s] for s in range(3)] for a in range(3)]
@@ -137,16 +145,15 @@
         total[1] * press[0] + total[0] * press[1],
         total[2] * press[0] + total[0] * press[2],
     ]
-    number = ps_ref[...].astype(F32)
-    slot_ref[...] = jnp.concatenate(
-        press + [wl[a][s] for s in range(3) for a in range(3)]
-        + [cell.astype(F32), number, jnp.zeros((2, SLOTS), F32)], 0
-    )
     sent = jnp.concatenate([number] + carry + total + [jnp.zeros((1, SLOTS), F32)], 0)
     for w in range(4):
         rows = exchange(sent[:, w * LANES:(w + 1) * LANES])
         for k in range(8):
             pay_ref[pl.ds((w * 8 + k) * BLOCK + ROWS_A, 1), :] = rows[k:k + 1]
+    slot_ref[...] = jnp.concatenate(
+        press + [wl[a][s] for s in range(3) for a in range(3)]
+        + [cell.astype(F32), number, jnp.zeros((2, SLOTS), F32)], 0
+    )
 
 
 def pack_kernel(p_ref, s_ref, ct_ref, t_ref, code_ref, sp_ref, st_ref, well_ref, link_ref, heel_ref,
@@ -182,7 +189,25 @@
     yhi_ref[...] = high
 
 
-def stencil_kernel(p_ref, s_ref, ct_ref, om_ref, pv_ref, t_ref, code_ref, bal_ref):
+def face(low, up, trans, code, direction):
+    return fluxes(
+        properties(low[0:3], low[3:6], low[6:9])[0], properties(up[0:3], up[3:6], up[6:9])[0],
+        low[0:3], up[0:3], trans, code, direction, None,
+    )
+
+
+def stencil_kernel(p_ref, s_ref, ct_ref, om_ref, pv_ref, t_ref, code_ref, slot_ref, xlo_ref, xhi_ref, exlo_ref, wxhi_ref,
+                   bal_ref, lane_hot_ref, row_hot_ref, seg_hot_ref):
+    cell = slot_ref[12:13, :].astype(jnp.int32)
+    lane_hot = jnp.where(iota((WIDE, SLOTS), 0) == (cell & (WIDE - 1)), 1.0, 0.0).T.astype(BF16)
+    lane_hot_ref[0:SLOTS, :] = lane_hot
+    lane_hot_ref[SLOTS:2 * SLOTS, :] = lane_hot
+    row_hot_ref[...] = one_hot(iota((WIDE_ROWS, SLOTS), 0) == (cell >> 8))
+    seg_lane = slot_ref[13:14, :].astype(jnp.int32) & (LANES - 1)
+    for w in range(4):
+        hot = one_hot(iota((LANES, LANES), 0) == seg_lane[:, w * LANES:(w + 1) * LANES])
+        seg_hot_ref[w, 0:LANES, :] = hot
+        seg_hot_ref[w, LANES:2 * LANES, :] = hot
     lane = iota((8, LANES), 1)
     sub = iota((8, LANES), 0)
     raw = nine(p_ref, s_ref, ct_ref, pl.ds(0, 8))
@@ -220,33 +245,41 @@
             for s in range(3):
                 bal_ref[s * 3 + a, at, :] = bal[a][s]
 
-
-def face(low, up, trans, code, direction):
-    return fluxes(
-        properties(low[0:3], low[3:6], low[6:9])[0], properties(up[0:3], up[3:6], up[6:9])[0],
-        low[0:3], up[0:3], trans, code, direction, None,
-    )
-
-
-def join_kernel(got_ref, slot_ref, bal_ref, seg_ref, xlo_ref, xhi_ref, ylo_ref, yhi_ref,
-                exlo_ref, wxhi_ref, nylo_ref, syhi_ref, res_ref, prod_ref, segout_ref):
+    top_x = lax.axis_index("xt") == TILES - 1
+    own, near = planes(xhi_ref, 11), planes(wxhi_ref, 11)
+    east = face(own[0:9], planes(exlo_ref, 9), jnp.where(top_x, 0.0, own[9]), own[10].astype(jnp.int32), 0)
+    west = face(near[0:9], planes(xlo_ref, 9), near[9], near[10].astype(jnp.int32), 0)
+    first, last = pl.ds(0, NZ, stride=8), pl.ds(7, NZ, stride=8)
+    for s in range(3):
+        for a in range(3):
+            n = s * 3 + a
+            bal_ref[n, last, :] = bal_ref[n, last, :] + east[a][s]
+            bal_ref[n, first, :] = bal_ref[n, first, :] - west[a][s]
+
+
+def join_kernel(got_ref, slot_ref, bal_ref, seg_ref, lane_hot_ref, row_hot_ref, seg_hot_ref, ylo_ref, yhi_ref,
+                nylo_ref, syhi_ref, exlo_ref, wxhi_ref, res_hbm, prod_hbm, segout_hbm, out_ref, segout_ref, sems):
     top_x = lax.axis_index("xt") == TILES - 1
     top_y = lax.axis_index("yt") == lax.axis_size("yt") - 1
     lane = iota((8, LANES), 1)
     group = iota((1, LANES), 1) >> 4
 
-    seg_number = slot_ref[13:14, :].astype(jnp.int32)
-    seg_lane = seg_number & (LANES - 1)
-    seg_row = seg_number >> 7
+    half = lane < 64
+    own_lo, own_hi, north, south = ylo_ref[...], yhi_ref[...], nylo_ref[...], syhi_ref[...]
+    low = [jnp.where(half, roll(own_hi, -8 * q, 1), roll(south, 64 - 8 * q, 1)) for q in range(11)]
+    up = [jnp.where(half, roll(north, -8 * q, 1), roll(own_lo, 64 - 8 * q, 1)) for q in range(9)]
+    trans = jnp.where(jnp.logical_and(half, top_y), 0.0, low[9])
+    rim = face(low[0:9], up, trans, low[10].astype(jnp.int32), 1)
+    even = (lane & 1) == 0
+    edge = jnp.logical_or(lane == 0, lane == LANES - 1)
+
+    seg_row = slot_ref[13:14, :].astype(jnp.int32) >> 7
     rates = [[] for _ in range(9)]
     for w in range(4):
         cols = slice(w * LANES, (w + 1) * LANES)
-        hot = one_hot(iota((LANES, LANES), 0) == seg_lane[:, cols])
         blocks = [got_ref[pl.ds((w * 8 + k) * BLOCK, ROWS_A), :] for k in range(8)]
         hi, lo = split(jnp.concatenate(blocks, 0))
-        picked = jnp.dot(
-            jnp.concatenate([hi, lo], 1), jnp.concatenate([hot, hot], 0), preferred_element_type=F32
-        )
+        picked = jnp.dot(jnp.concatenate([hi, lo], 1), seg_hot_ref[w], preferred_element_type=F32)
         mine = picked[0:ROWS_A]
         for k in range(1, 8):
             mine = jnp.where(group == k, picked[k * ROWS_A:(k + 1) * ROWS_A], mine)
@@ -262,47 +295,30 @@
                 r = 3 + s * 3 + a
                 rates[s * 3 + a].append(slot_ref[r:r + 1, cols] * drop[0] + base[a] * drop[s])
 
-    cell = slot_ref[12:13, :].astype(jnp.int32)
-    lane_hot = one_hot(iota((LANES, SLOTS), 0) == (cell & (LANES - 1)))
-    row_hot = one_hot(iota((CELL_ROWS, SLOTS), 0) == (cell >> 7))
+    row_hot = row_hot_ref[...]
     parts = [split(jnp.concatenate(r, 1)) for r in rates]
-    left = jnp.concatenate(
-        [jnp.concatenate([row_hot * hi, row_hot * lo], 1) for hi, lo in parts], 0
-    )
-    added = lax.dot_general(
-        left, jnp.concatenate([lane_hot, lane_hot], 1), (((1,), (1,)), ((), ())), preferred_element_type=F32
-    )
-
-    half = lane < 64
-    own_lo, own_hi, north, south = ylo_ref[...], yhi_ref[...], nylo_ref[...], syhi_ref[...]
-    low = [jnp.where(half, roll(own_hi, -8 * q, 1), roll(south, 64 - 8 * q, 1)) for q in range(11)]
-    up = [jnp.where(half, roll(north, -8 * q, 1), roll(own_lo, 64 - 8 * q, 1)) for q in range(9)]
-    trans = jnp.where(jnp.logical_and(half, top_y), 0.0, low[9])
-    rim = face(low[0:9], up, trans, low[10].astype(jnp.int32), 1)
-    even = (lane & 1) == 0
-    edge = jnp.logical_or(lane == 0, lane == LANES - 1)
-
-    def planes(ref, count):
-        return [ref[q * 8:(q + 1) * 8, :] for q in range(count)]
-
-    own, near = planes(xhi_ref, 11), planes(wxhi_ref, 11)
-    east = face(own[0:9], planes(exlo_ref, 9), jnp.where(top_x, 0.0, own[9]), own[10].astype(jnp.int32), 0)
-    west = face(near[0:9], planes(xlo_ref, 9), near[9], near[10].astype(jnp.int32), 0)
-    first, last = pl.ds(0, NZ, stride=8), pl.ds(7, NZ, stride=8)
-
+    left = jnp.concatenate([jnp.concatenate([row_hot * hi, row_hot * lo], 1) for hi, lo in parts], 0)
+    added = jnp.dot(left, lane_hot_ref[...], preferred_element_type=F32)
+    copies = []
     for s in range(3):
         for a in range(3):
             n = s * 3 + a
             flux = rim[a][s]
             moved = roll(flux, 65, 1)
             by_parity = (jnp.where(even, flux, -moved), jnp.where(even, -moved, flux))
-            out = res_ref.at[a] if s == 0 else prod_ref.at[s - 1, a]
             for z in range(NZ):
                 at = pl.ds(z * 8, 8)
-                rim_z = jnp.where(edge, roll(by_parity[z % 2], LANES - 1 - z, 1), 0.0)
-                out[at, :] = bal_ref[n, at, :] + added[n * CELL_ROWS + z * 8:n * CELL_ROWS + z * 8 + 8] + rim_z
-            out[last, :] = out[last, :] + east[a][s]
-            out[first, :] = out[first, :] - west[a][s]
+                out_ref[n, at, :] = bal_ref[n, at, :] + jnp.where(
+                    edge, roll(by_parity[z % 2], LANES - 1 - z, 1), 0.0
+                )
+            for h in range(2):
+                at = pl.ds(h, WIDE_ROWS, stride=2)
+                more = added[n * WIDE_ROWS:(n + 1) * WIDE_ROWS, h * LANES:(h + 1) * LANES]
+                out_ref[n, at, :] = out_ref[n, at, :] + more
+        copies.append(pltpu.make_async_copy(
+            out_ref.at[pl.ds(s * 3, 3)], res_hbm if s == 0 else prod_hbm.at[s - 1], sems.at[s]
+        ))
+        copies[-1].start()
 
     told = jnp.concatenate(
         [exchange(got_ref[pl.ds(w * 8 * BLOCK + ROWS_A, 8, stride=BLOCK), :]) for w in range(4)], 1
@@ -338,23 +354,30 @@
         carried = jnp.where(linked, flow, 0.0)
         entering = jnp.where(joined, link_west * (roll(before, 3 + s, 1) - seg[s]), 0.0)
         segout_ref[s] = inflow[s] - flow + jnp.where(lane0, entering, roll(carried, 1, 1))
-
-
-def call(kernel, out_shapes, *args, in_spec=VMEM, scratch=()):
+    copies.append(pltpu.make_async_copy(segout_ref, segout_hbm, sems.at[3]))
+    copies[-1].start()
+    for copy in copies:
+        copy.wait()
+
+
+HBM = pl.BlockSpec(memory_space=pltpu.HBM)
+
+
+def call(kernel, outs, *args, in_spec=VMEM, out_spec=VMEM, scratch=()):
     return pl.pallas_call(
         kernel,
-        out_shape=[jax.ShapeDtypeStruct(s, F32) for s in out_shapes],
+        out_shape=[jax.ShapeDtypeStruct(o, F32) if isinstance(o, tuple) else o for o in outs],
         in_specs=[in_spec] * len(args),
-        out_specs=[VMEM] * len(out_shapes),
+        out_specs=[out_spec] * len(outs),
         scratch_shapes=scratch,
         compiler_params=pltpu.CompilerParams(vmem_limit_bytes=16 * 2**20),
     )(*args)
 
 
-def call_loading(kernel, out_shapes, *args):
+def call_loading(kernel, outs, *args):
     scratch = [pltpu.VMEM(a.shape, a.dtype) for a in args] + [pltpu.SemaphoreType.DMA((len(args),))]
     args = [pltpu.with_memory_space_constraint(a, pltpu.HBM) for a in args]
-    return call(kernel, out_shapes, *args, in_spec=pl.BlockSpec(memory_space=pltpu.HBM), scratch=scratch)
+    return call(kernel, outs, *args, in_spec=HBM, scratch=scratch)
 
 
 def shift(array, axis, by):
@@ -390,10 +413,17 @@
     east_xlo = shift(xlo, "xt", -1)
     north_ylo = shift(ylo, "yt", -1)
     south_yhi = shift(yhi, "yt", 1)
-    (bal,) = call(stencil_kernel, [(9, CELL_ROWS, LANES)], p, sat, ct, om, pv, tr, code)
+    bal, lane_hot, row_hot, seg_hot = call(
+        stencil_kernel,
+        [(9, CELL_ROWS, LANES), jax.ShapeDtypeStruct((2 * SLOTS, WIDE), BF16),
+         jax.ShapeDtypeStruct((WIDE_ROWS, SLOTS), BF16), jax.ShapeDtypeStruct((4, 2 * LANES, LANES), BF16)],
+        p, sat, ct, om, pv, tr, code, slots, xlo, xhi, east_xlo, west_xhi,
+    )
     res, prod, seg = call(
         join_kernel, [(3, CELL_ROWS, LANES), (2, 3, CELL_ROWS, LANES), (3, 8, LANES)],
-        got, slots, bal, seg, xlo, xhi, ylo, yhi, east_xlo, west_xhi, north_ylo, south_yhi,
+        got, slots, bal, seg, lane_hot, row_hot, seg_hot, ylo, yhi, north_ylo, south_yhi, east_xlo, west_xhi,
+        out_spec=HBM,
+        scratch=[pltpu.VMEM((9, CELL_ROWS, LANES), F32), pltpu.VMEM((3, 8, LANES), F32), pltpu.SemaphoreType.DMA((4,))],
     )
     return (res.reshape(old_mass.shape), prod.reshape(cell_tangent.shape), seg)
 

time: 34.7 us -> 34.7 us (level)
  waiting for transfers between devices: 6.29 us -> 5.91 us
  Pallas kernels: 4.49 us -> 4.84 us
    ppermute x4, waiting for transfers between devices: 2.13 us -> 1.76 us  [shift(): lax.ppermute(array, axis, [(i, i + by) for i in range(length) if 0 <= i +...]
    pallas_call x4, Pallas kernels: 4.49 us -> 4.84 us  [call(): pl.pallas_call(kernel, out_shape=[jax.ShapeDtypeStruct(o, F32) if isinsta...]
  transfers between devices with their start and end apart: 5 -> 5, of which waited for: 2 -> 3; matrix products, arithmetic and copies ran while one was open for 0% -> 0% of each run, Pallas kernels for 2% -> 3%
where the time goes in v3:
time: 34.7 us; the launch traced here: 34.3 us
  starting transfers between devices  22.6 us (65%)
  waiting for transfers between devices  5.91 us (17%)
  Pallas kernels  4.84 us (14%)
  between operations  0.88 us (3%)
    all_to_all x1, starting transfers between devices, body(): lax.all_to_all(pay.reshape(TILES, 1, BLOCK * LANES), 'xt', 0, 0, tiled=True)  13.3 us
    ppermute x4, starting transfers between devices, shift(): lax.ppermute(array, axis, [(i, i + by) for i in range(length) if 0 <= i +...  9.31 us
    pallas_call x4, Pallas kernels, call(): pl.pallas_call(kernel, out_shape=[jax.ShapeDtypeStruct(o, F32) if isinsta...  4.84 us
    all_to_all x1, waiting for transfers between devices, body(): lax.all_to_all(pay.reshape(TILES, 1, BLOCK * LANES), 'xt', 0, 0, tiled=True)  4.15 us
    ppermute x4, waiting for transfers between devices, shift(): lax.ppermute(array, axis, [(i, i + by) for i in range(length) if 0 <= i +...  1.76 us
  transfers between devices with their start and end apart: 5, of which 3 were waited for; matrix products, arithmetic and copies ran while one was open for 0% of the time, Pallas kernels for 3%

profile of v3, /device:TPU:56, one launch (start us, length us, event | category | flops | bytes accessed | tf_op | source)
XLA Modules:
  0.0 34.3 jit_solution(5842147585952688610)
XLA Ops:
  0.6 2.5 %shard_map.175 = (f32[800,128]{1,0:T(8,128)}, f32[16,512]{1,0:T(8,128)S(1)}) custom-call(f32[64,128]{1,0:T(8,128)} %bitcast.20, f32[2,64,128]{2,1,0:T(8,128)} %bitcast.15, f32[2,3,64,128]{3,2,1,0:T(8,128)} %bitcast.11, f32[8,128]{1,0:T(8,128)} %sp_ref.1, f32[2,8,128]{2,1,0:T(8,128)} %st_ref.1, s32[1,512]{1,0:T(1,128)} %pc_hbm.1, s32[1,512]{1,0:T(1,128)} %ps_hbm.1, ...), custom_call_target="tpu_custom_call" | custom-call | tf_op jit(solution)/shard_map/pallas_call | solution.py:367
  3.1 0.0 copy-start
  3.1 0.0 copy-start.1
  3.1 0.0 copy-start.2
  3.2 0.0 copy-start.3
  3.2 0.0 copy-start.4
  3.2 0.0 copy-start.6
  3.2 0.0 copy-start.8
  3.2 0.0 copy-start.9
  3.2 0.0 copy-start.10
  3.2 0.0 copy-start.11
  3.2 13.3 %all-to-all-start = ((f32[32,1,3200]{2,1,0:T(1,128)}), f32[32,1,3200]{2,1,0:T(1,128)S(1)}, u32[]{:S(2)}, u32[]{:S(2)}) async-start(f32[32,1,3200]{2,1,0:T(1,128)} %bitcast.3), calls=%async_computation | async-start | bytes 819200 | tf_op jit(solution)/shard_map/all_to_all | solution.py:406
  16.6 0.0 copy-done
  16.6 0.0 copy-done.1
  16.6 0.0 copy-done.2
  16.6 0.0 copy-done.3
  16.6 0.0 copy-done.4
  16.6 0.0 copy-done.6
  16.6 0.0 copy-done.8
  16.6 0.0 copy-done.9
  16.6 0.0 copy-done.10
  16.7 0.0 copy-done.11
  16.7 0.0 copy-start.5
  16.7 0.0 copy-start.7
  16.7 0.2 shard_map.176
  16.9 3.7 %collective-permute-start.1 = (f32[96,128]{1,0:T(8,128)S(1)}, f32[96,128]{1,0:T(8,128)S(1)}, u32[]{:S(2)}, u32[]{:S(2)}) collective-permute-start(f32[96,128]{1,0:T(8,128)S(1)} %get-tuple-element.20.xhi_ref), channel_id=1, source_target_pairs={{0,16},{16,32},{32,48},{48,64},{64,80},{80,96},{96,112},{112,128},... | collective-permute-start | bytes 147464 | tf_op jit(solution)/shard_map/ppermute | solution.py:385
  20.6 1.3 %collective-permute-start = (f32[80,128]{1,0:T(8,128)S(1)}, f32[80,128]{1,0:T(8,128)S(1)}, u32[]{:S(2)}, u32[]{:S(2)}) collective-permute-start(f32[80,128]{1,0:T(8,128)S(1)} %get-tuple-element.19.xlo_ref), channel_id=1, source_target_pairs={{16,0},{32,16},{48,32},{64,48},{80,64},{96,80},{112,96},{128,112},... | collective-permute-start | bytes 122888 | tf_op jit(solution)/shard_map/ppermute | solution.py:385
  21.9 1.9 %collective-permute-start.2 = (f32[8,128]{1,0:T(8,128)S(1)}, f32[8,128]{1,0:T(8,128)S(1)}, u32[]{:S(2)}, u32[]{:S(2)}) collective-permute-start(f32[8,128]{1,0:T(8,128)S(1)} %get-tuple-element.26.ylo_ref), channel_id=1, source_target_pairs={{1,0},{2,1},{3,2},{4,3},{5,4},{6,5},{7,6},{8,7},{9,8},{10,9},{11,1... | collective-permute-start | bytes 12296 | tf_op jit(solution)/shard_map/ppermute | solution.py:385
  23.9 2.4 %collective-permute-start.3 = (f32[8,128]{1,0:T(8,128)S(1)}, f32[8,128]{1,0:T(8,128)S(1)}, u32[]{:S(2)}, u32[]{:S(2)}) collective-permute-start(f32[8,128]{1,0:T(8,128)S(1)} %get-tuple-element.27.yhi_ref), channel_id=1, source_target_pairs={{0,1},{1,2},{2,3},{3,4},{4,5},{5,6},{6,7},{7,8},{8,9},{9,10},{10,1... | collective-permute-start | bytes 12296 | tf_op jit(solution)/shard_map/ppermute | solution.py:385
  26.3 0.5 %collective-permute-done.exlo_ref = f32[80,128]{1,0:T(8,128)S(1)} collective-permute-done((f32[80,128]{1,0:T(8,128)S(1)}, f32[80,128]{1,0:T(8,128)S(1)}, u32[]{:S(2)}, u32[]{:S(2)}) %collective-permute-start) | collective-permute-done | bytes 40992 | tf_op jit(solution)/shard_map/ppermute | solution.py:385
  26.8 0.0 collective-permute-done.1.wxhi_ref
  26.8 0.0 copy-done.5
  26.8 0.0 copy-done.7
  26.8 0.7 %shard_map.177 = (f32[9,64,128]{2,1,0:T(8,128)S(1)}, bf16[1024,256]{1,0:T(8,128)(2,1)S(1)}, bf16[32,512]{1,0:T(8,128)(2,1)S(1)}, bf16[4,256,128]{2,1,0:T(8,128)(2,1)S(1)}) custom-call(f32[64,128]{1,0:T(8,128)S(1)} %bitcast.22, f32[2,64,128]{2,1,0:T(8,128)S(1)} %bitcast.17, f32[2,3,64,128]{3,2,1,0:T(8,128)S(1)} %bitcast.13, f32[3,64,128]{2,1,0:T(8,128)S(1)} %bitcast.25, ...), custom_call_target="tpu_custom_call" | custom-call | tf_op jit(solution)/shard_map/pallas_call | solution.py:367
  27.5 0.0 collective-permute-done.2.nylo_ref
  27.5 1.3 %collective-permute-done.3.syhi_ref = f32[8,128]{1,0:T(8,128)S(1)} collective-permute-done((f32[8,128]{1,0:T(8,128)S(1)}, f32[8,128]{1,0:T(8,128)S(1)}, u32[]{:S(2)}, u32[]{:S(2)}) %collective-permute-start.3) | collective-permute-done | bytes 4128 | tf_op jit(solution)/shard_map/ppermute | solution.py:385
  28.8 4.1 %all-to-all-done = f32[32,1,3200]{2,1,0:T(1,128)S(1)} async-done(((f32[32,1,3200]{2,1,0:T(1,128)}), f32[32,1,3200]{2,1,0:T(1,128)S(1)}, u32[]{:S(2)}, u32[]{:S(2)}) %all-to-all-start) | async-done | bytes 409632 | tf_op jit(solution)/shard_map/all_to_all | solution.py:406
  33.0 1.4 %shard_map.178 = (f32[3,64,128]{2,1,0:T(8,128)}, f32[2,3,64,128]{3,2,1,0:T(8,128)}, f32[3,8,128]{2,1,0:T(8,128)}) custom-call(f32[800,128]{1,0:T(8,128)S(1)} %bitcast.14, f32[16,512]{1,0:T(8,128)S(1)} %get-tuple-element.18.slot_ref, f32[9,64,128]{2,1,0:T(8,128)S(1)} %get-tuple-element.21.bal_ref, f32[48,128]{1,0:T(8,128)S(1)} %get-tuple-element.22.seg_ref, ...), custom_call_target="tpu_custom_call" | custom-call | tf_op jit(solution)/shard_map/pallas_call | solution.py:367
Async XLA Ops:
  3.1 13.4 %copy-start = (f32[2,3,8,8,128]{4,3,2,1,0:T(8,128)S(1)}, f32[2,3,8,8,128]{4,3,2,1,0:T(8,128)}, u32[]{:S(2)}) copy-start(f32[2,3,8,8,128]{4,3,2,1,0:T(8,128)} %param.22) | copy-start | bytes 589828
  3.1 13.4 %copy-start.1 = (f32[2,8,8,128]{3,2,1,0:T(8,128)S(1)}, f32[2,8,8,128]{3,2,1,0:T(8,128)}, u32[]{:S(2)}) copy-start(f32[2,8,8,128]{3,2,1,0:T(8,128)} %param.17) | copy-start | bytes 196612
  3.1 13.4 %copy-start.2 = (f32[3,8,8,128]{3,2,1,0:T(8,128)S(1)}, f32[3,8,8,128]{3,2,1,0:T(8,128)}, u32[]{:S(2)}) copy-start(f32[3,8,8,128]{3,2,1,0:T(8,128)} %param.20) | copy-start | bytes 294916
  3.2 13.4 %copy-start.3 = (f32[8,8,128]{2,1,0:T(8,128)S(1)}, f32[8,8,128]{2,1,0:T(8,128)}, u32[]{:S(2)}) copy-start(f32[8,8,128]{2,1,0:T(8,128)} %param.16) | copy-start | bytes 98308
  3.2 13.4 %copy-start.4 = (s32[8,8,128]{2,1,0:T(8,128)S(1)}, s32[8,8,128]{2,1,0:T(8,128)}, u32[]{:S(2)}) copy-start(s32[8,8,128]{2,1,0:T(8,128)} %param.21) | copy-start | bytes 98308
  3.2 13.4 %copy-start.6 = (f32[2,8,128]{2,1,0:T(8,128)S(1)}, f32[2,8,128]{2,1,0:T(8,128)}, u32[]{:S(2)}) copy-start(f32[2,8,128]{2,1,0:T(8,128)} %st_ref.1) | copy-start | bytes 24580
  3.2 13.4 %copy-start.8 = (f32[8,128]{1,0:T(8,128)S(1)}, f32[8,128]{1,0:T(8,128)}, u32[]{:S(2)}) copy-start(f32[8,128]{1,0:T(8,128)} %sp_ref.1) | copy-start | bytes 12292
  3.2 13.4 %copy-start.9 = (s32[8,128]{1,0:T(8,128)S(1)}, s32[8,128]{1,0:T(8,128)}, u32[]{:S(2)}) copy-start(s32[8,128]{1,0:T(8,128)} %well_ref.1) | copy-start | bytes 12292
  3.2 13.4 %copy-start.10 = (f32[8,128]{1,0:T(8,128)S(1)}, f32[8,128]{1,0:T(8,128)}, u32[]{:S(2)}) copy-start(f32[8,128]{1,0:T(8,128)} %link_ref.1) | copy-start | bytes 12292
  3.2 13.4 %copy-start.11 = (f32[8,128]{1,0:T(8,128)S(1)}, f32[8,128]{1,0:T(8,128)}, u32[]{:S(2)}) copy-start(f32[8,128]{1,0:T(8,128)} %heel_ref.1) | copy-start | bytes 12292
  3.2 29.7 %all-to-all-start = ((f32[32,1,3200]{2,1,0:T(1,128)}), f32[32,1,3200]{2,1,0:T(1,128)S(1)}, u32[]{:S(2)}, u32[]{:S(2)}) async-start(f32[32,1,3200]{2,1,0:T(1,128)} %bitcast.3), calls=%async_computation | async-start | bytes 819200 | tf_op jit(solution)/shard_map/all_to_all | solution.py:406
  16.7 10.1 %copy-start.5 = (f32[3,8,8,128]{3,2,1,0:T(8,128)S(1)}, f32[3,8,8,128]{3,2,1,0:T(8,128)}, u32[]{:S(2)}) copy-start(f32[3,8,8,128]{3,2,1,0:T(8,128)} %param.18) | copy-start | bytes 294916
  16.7 10.1 %copy-start.7 = (f32[8,8,128]{2,1,0:T(8,128)S(1)}, f32[8,8,128]{2,1,0:T(8,128)}, u32[]{:S(2)}) copy-start(f32[8,8,128]{2,1,0:T(8,128)} %param.19) | copy-start | bytes 98308
  16.9 9.8 %collective-permute-start.1 = (f32[96,128]{1,0:T(8,128)S(1)}, f32[96,128]{1,0:T(8,128)S(1)}, u32[]{:S(2)}, u32[]{:S(2)}) collective-permute-start(f32[96,128]{1,0:T(8,128)S(1)} %get-tuple-element.20.xhi_ref), channel_id=1, source_target_pairs={{0,16},{16,32},{32,48},{48,64},{64,80},{80,96},{96,112},{112,128},... | collective-permute-start | bytes 147464 | tf_op jit(solution)/shard_map/ppermute | solution.py:385
  20.6 6.1 %collective-permute-start = (f32[80,128]{1,0:T(8,128)S(1)}, f32[80,128]{1,0:T(8,128)S(1)}, u32[]{:S(2)}, u32[]{:S(2)}) collective-permute-start(f32[80,128]{1,0:T(8,128)S(1)} %get-tuple-element.19.xlo_ref), channel_id=1, source_target_pairs={{16,0},{32,16},{48,32},{64,48},{80,64},{96,80},{112,96},{128,112},... | collective-permute-start | bytes 122888 | tf_op jit(solution)/shard_map/ppermute | solution.py:385
  21.9 5.6 %collective-permute-start.2 = (f32[8,128]{1,0:T(8,128)S(1)}, f32[8,128]{1,0:T(8,128)S(1)}, u32[]{:S(2)}, u32[]{:S(2)}) collective-permute-start(f32[8,128]{1,0:T(8,128)S(1)} %get-tuple-element.26.ylo_ref), channel_id=1, source_target_pairs={{1,0},{2,1},{3,2},{4,3},{5,4},{6,5},{7,6},{8,7},{9,8},{10,9},{11,1... | collective-permute-start | bytes 12296 | tf_op jit(solution)/shard_map/ppermute | solution.py:385
  23.9 4.9 %collective-permute-start.3 = (f32[8,128]{1,0:T(8,128)S(1)}, f32[8,128]{1,0:T(8,128)S(1)}, u32[]{:S(2)}, u32[]{:S(2)}) collective-permute-start(f32[8,128]{1,0:T(8,128)S(1)} %get-tuple-element.27.yhi_ref), channel_id=1, source_target_pairs={{0,1},{1,2},{2,3},{3,4},{4,5},{5,6},{6,7},{7,8},{8,9},{9,10},{10,1... | collective-permute-start | bytes 12296 | tf_op jit(solution)/shard_map/ppermute | solution.py:385

commit v4 on v3

--- a/solution.py
+++ b/solution.py
@@ -18,6 +18,8 @@
 ROWS_A = 24
 BLOCK = ROWS_A + 1
 WIDE = 256
+ORDER = [r // 2 + TILES // 2 * (r % 2) for r in range(TILES)]
+PLACE = [ORDER.index(k) for k in range(TILES)]
 WIDE_ROWS = 32
 F32 = jnp.float32
 BF16 = jnp.bfloat16
@@ -149,7 +151,7 @@
     for w in range(4):
         rows = exchange(sent[:, w * LANES:(w + 1) * LANES])
         for k in range(8):
-            pay_ref[pl.ds((w * 8 + k) * BLOCK + ROWS_A, 1), :] = rows[k:k + 1]
+            pay_ref[pl.ds(PLACE[w * 8 + k] * BLOCK + ROWS_A, 1), :] = rows[k:k + 1]
     slot_ref[...] = jnp.concatenate(
         press + [wl[a][s] for s in range(3) for a in range(3)]
         + [cell.astype(F32), number, jnp.zeros((2, SLOTS), F32)], 0
@@ -277,7 +279,7 @@
     rates = [[] for _ in range(9)]
     for w in range(4):
         cols = slice(w * LANES, (w + 1) * LANES)
-        blocks = [got_ref[pl.ds((w * 8 + k) * BLOCK, ROWS_A), :] for k in range(8)]
+        blocks = [got_ref[pl.ds(PLACE[w * 8 + k] * BLOCK, ROWS_A), :] for k in range(8)]
         hi, lo = split(jnp.concatenate(blocks, 0))
         picked = jnp.dot(jnp.concatenate([hi, lo], 1), seg_hot_ref[w], preferred_element_type=F32)
         mine = picked[0:ROWS_A]
@@ -403,7 +405,9 @@
         p, sat, ct, segment_pressure, segment_tangent, perforation_cell, perforation_segment, well_index,
         perforation_count,
     )
-    got = lax.all_to_all(pay.reshape(TILES, 1, BLOCK * LANES), "xt", 0, 0, tiled=True)
+    got = lax.all_to_all(
+        pay.reshape(TILES, 1, BLOCK * LANES), "xt", 0, 0, tiled=True, axis_index_groups=[ORDER]
+    )
     got = got.reshape(TILES * BLOCK, LANES)
     xlo, xhi, ylo, yhi, seg = call(
         pack_kernel, [(80, LANES), (96, LANES), (8, LANES), (8, LANES), (48, LANES)],

time: 34.7 us -> 34.1 us (0.983)
  the two profiles are of different devices: /device:TPU:56 before, /device:TPU:96 now
where the time goes in v4:
time: 34.1 us; the launch traced here: 33.8 us
  starting transfers between devices  25 us (73%)
  Pallas kernels  4.83 us (14%)
  waiting for transfers between devices  2.94 us (9%)
  between operations  0.9 us (3%)
    all_to_all x1, starting transfers between devices, body(): lax.all_to_all(pay.reshape(TILES, 1, BLOCK * LANES), 'xt', 0, 0, tiled=Tr...  12.7 us
    ppermute x4, starting transfers between devices, shift(): lax.ppermute(array, axis, [(i, i + by) for i in range(length) if 0 <= i +...  12.3 us
    pallas_call x4, Pallas kernels, call(): pl.pallas_call(kernel, out_shape=[jax.ShapeDtypeStruct(o, F32) if isinsta...  4.83 us
    ppermute x4, waiting for transfers between devices, shift(): lax.ppermute(array, axis, [(i, i + by) for i in range(length) if 0 <= i +...  2.94 us
  transfers between devices with their start and end apart: 5, of which 1 were waited for; matrix products, arithmetic and copies ran while one was open for 0% of the time, Pallas kernels for 3%

profile of v4, /device:TPU:96, one launch (start us, length us, event | category | flops | bytes accessed | tf_op | source)
XLA Modules:
  0.0 33.8 jit_solution(7923233696834674891)
XLA Ops:
  0.6 2.5 %shard_map.175 = (f32[800,128]{1,0:T(8,128)}, f32[16,512]{1,0:T(8,128)S(1)}) custom-call(f32[64,128]{1,0:T(8,128)} %bitcast.20, f32[2,64,128]{2,1,0:T(8,128)} %bitcast.15, f32[2,3,64,128]{3,2,1,0:T(8,128)} %bitcast.11, f32[8,128]{1,0:T(8,128)} %sp_ref.1, f32[2,8,128]{2,1,0:T(8,128)} %st_ref.1, s32[1,512]{1,0:T(1,128)} %pc_hbm.1, s32[1,512]{1,0:T(1,128)} %ps_hbm.1, ...), custom_call_target="tpu_custom_call" | custom-call | tf_op jit(solution)/shard_map/pallas_call | solution.py:369
  3.1 0.0 copy-start
  3.1 0.0 copy-start.1
  3.1 0.0 copy-start.2
  3.2 0.0 copy-start.3
  3.2 0.0 copy-start.4
  3.2 0.0 copy-start.6
  3.2 0.0 copy-start.8
  3.2 0.0 copy-start.9
  3.2 0.0 copy-start.10
  3.2 0.0 copy-start.11
  3.2 12.7 %all-to-all-start = ((f32[32,1,3200]{2,1,0:T(1,128)}), f32[32,1,3200]{2,1,0:T(1,128)S(1)}, u32[]{:S(2)}, u32[]{:S(2)}) async-start(f32[32,1,3200]{2,1,0:T(1,128)} %bitcast.3), calls=%async_computation | async-start | bytes 819200 | tf_op jit(solution)/shard_map/all_to_all | solution.py:408
  16.0 0.0 copy-done
  16.0 0.0 copy-done.1
  16.0 0.0 copy-done.2
  16.0 0.0 copy-done.3
  16.0 0.0 copy-done.4
  16.0 0.0 copy-done.6
  16.0 0.0 copy-done.8
  16.1 0.0 copy-done.9
  16.1 0.0 copy-done.10
  16.1 0.0 copy-done.11
  16.1 0.0 copy-start.5
  16.1 0.0 copy-start.7
  16.1 0.2 shard_map.176
  16.4 3.4 %collective-permute-start.1 = (f32[96,128]{1,0:T(8,128)S(1)}, f32[96,128]{1,0:T(8,128)S(1)}, u32[]{:S(2)}, u32[]{:S(2)}) collective-permute-start(f32[96,128]{1,0:T(8,128)S(1)} %get-tuple-element.20.xhi_ref), channel_id=1, source_target_pairs={{0,16},{16,32},{32,48},{48,64},{64,80},{80,96},{96,112},{112,128},... | collective-permute-start | bytes 147464 | tf_op jit(solution)/shard_map/ppermute | solution.py:387
  19.7 4.6 %collective-permute-start = (f32[80,128]{1,0:T(8,128)S(1)}, f32[80,128]{1,0:T(8,128)S(1)}, u32[]{:S(2)}, u32[]{:S(2)}) collective-permute-start(f32[80,128]{1,0:T(8,128)S(1)} %get-tuple-element.19.xlo_ref), channel_id=1, source_target_pairs={{16,0},{32,16},{48,32},{64,48},{80,64},{96,80},{112,96},{128,112},... | collective-permute-start | bytes 122888 | tf_op jit(solution)/shard_map/ppermute | solution.py:387
  24.3 1.9 %collective-permute-start.2 = (f32[8,128]{1,0:T(8,128)S(1)}, f32[8,128]{1,0:T(8,128)S(1)}, u32[]{:S(2)}, u32[]{:S(2)}) collective-permute-start(f32[8,128]{1,0:T(8,128)S(1)} %get-tuple-element.26.ylo_ref), channel_id=1, source_target_pairs={{1,0},{2,1},{3,2},{4,3},{5,4},{6,5},{7,6},{8,7},{9,8},{10,9},{11,1... | collective-permute-start | bytes 12296 | tf_op jit(solution)/shard_map/ppermute | solution.py:387
  26.3 2.4 %collective-permute-start.3 = (f32[8,128]{1,0:T(8,128)S(1)}, f32[8,128]{1,0:T(8,128)S(1)}, u32[]{:S(2)}, u32[]{:S(2)}) collective-permute-start(f32[8,128]{1,0:T(8,128)S(1)} %get-tuple-element.27.yhi_ref), channel_id=1, source_target_pairs={{0,1},{1,2},{2,3},{3,4},{4,5},{5,6},{6,7},{7,8},{8,9},{9,10},{10,1... | collective-permute-start | bytes 12296 | tf_op jit(solution)/shard_map/ppermute | solution.py:387
  28.7 0.0 collective-permute-done.exlo_ref
  28.7 0.0 collective-permute-done.1.wxhi_ref
  28.7 0.0 copy-done.5
  28.7 0.0 copy-done.7
  28.7 0.7 %shard_map.177 = (f32[9,64,128]{2,1,0:T(8,128)S(1)}, bf16[1024,256]{1,0:T(8,128)(2,1)S(1)}, bf16[32,512]{1,0:T(8,128)(2,1)S(1)}, bf16[4,256,128]{2,1,0:T(8,128)(2,1)S(1)}) custom-call(f32[64,128]{1,0:T(8,128)S(1)} %bitcast.22, f32[2,64,128]{2,1,0:T(8,128)S(1)} %bitcast.17, f32[2,3,64,128]{3,2,1,0:T(8,128)S(1)} %bitcast.13, f32[3,64,128]{2,1,0:T(8,128)S(1)} %bitcast.25, ...), custom_call_target="tpu_custom_call" | custom-call | tf_op jit(solution)/shard_map/pallas_call | solution.py:369
  29.5 0.0 collective-permute-done.2.nylo_ref
  29.5 2.9 %collective-permute-done.3.syhi_ref = f32[8,128]{1,0:T(8,128)S(1)} collective-permute-done((f32[8,128]{1,0:T(8,128)S(1)}, f32[8,128]{1,0:T(8,128)S(1)}, u32[]{:S(2)}, u32[]{:S(2)}) %collective-permute-start.3) | collective-permute-done | bytes 4128 | tf_op jit(solution)/shard_map/ppermute | solution.py:387
  32.4 0.0 all-to-all-done
  32.4 1.4 %shard_map.178 = (f32[3,64,128]{2,1,0:T(8,128)}, f32[2,3,64,128]{3,2,1,0:T(8,128)}, f32[3,8,128]{2,1,0:T(8,128)}) custom-call(f32[800,128]{1,0:T(8,128)S(1)} %bitcast.14, f32[16,512]{1,0:T(8,128)S(1)} %get-tuple-element.18.slot_ref, f32[9,64,128]{2,1,0:T(8,128)S(1)} %get-tuple-element.21.bal_ref, f32[48,128]{1,0:T(8,128)S(1)} %get-tuple-element.22.seg_ref, ...), custom_call_target="tpu_custom_call" | custom-call | tf_op jit(solution)/shard_map/pallas_call | solution.py:369
Async XLA Ops:
  3.1 12.9 %copy-start = (f32[2,3,8,8,128]{4,3,2,1,0:T(8,128)S(1)}, f32[2,3,8,8,128]{4,3,2,1,0:T(8,128)}, u32[]{:S(2)}) copy-start(f32[2,3,8,8,128]{4,3,2,1,0:T(8,128)} %param.22) | copy-start | bytes 589828
  3.1 12.9 %copy-start.1 = (f32[2,8,8,128]{3,2,1,0:T(8,128)S(1)}, f32[2,8,8,128]{3,2,1,0:T(8,128)}, u32[]{:S(2)}) copy-start(f32[2,8,8,128]{3,2,1,0:T(8,128)} %param.17) | copy-start | bytes 196612
  3.1 12.9 %copy-start.2 = (f32[3,8,8,128]{3,2,1,0:T(8,128)S(1)}, f32[3,8,8,128]{3,2,1,0:T(8,128)}, u32[]{:S(2)}) copy-start(f32[3,8,8,128]{3,2,1,0:T(8,128)} %param.20) | copy-start | bytes 294916
  3.2 12.9 %copy-start.3 = (f32[8,8,128]{2,1,0:T(8,128)S(1)}, f32[8,8,128]{2,1,0:T(8,128)}, u32[]{:S(2)}) copy-start(f32[8,8,128]{2,1,0:T(8,128)} %param.16) | copy-start | bytes 98308
  3.2 12.9 %copy-start.4 = (s32[8,8,128]{2,1,0:T(8,128)S(1)}, s32[8,8,128]{2,1,0:T(8,128)}, u32[]{:S(2)}) copy-start(s32[8,8,128]{2,1,0:T(8,128)} %param.21) | copy-start | bytes 98308
  3.2 12.8 %copy-start.6 = (f32[2,8,128]{2,1,0:T(8,128)S(1)}, f32[2,8,128]{2,1,0:T(8,128)}, u32[]{:S(2)}) copy-start(f32[2,8,128]{2,1,0:T(8,128)} %st_ref.1) | copy-start | bytes 24580
  3.2 12.8 %copy-start.8 = (f32[8,128]{1,0:T(8,128)S(1)}, f32[8,128]{1,0:T(8,128)}, u32[]{:S(2)}) copy-start(f32[8,128]{1,0:T(8,128)} %sp_ref.1) | copy-start | bytes 12292
  3.2 12.8 %copy-start.9 = (s32[8,128]{1,0:T(8,128)S(1)}, s32[8,128]{1,0:T(8,128)}, u32[]{:S(2)}) copy-start(s32[8,128]{1,0:T(8,128)} %well_ref.1) | copy-start | bytes 12292
  3.2 12.8 %copy-start.10 = (f32[8,128]{1,0:T(8,128)S(1)}, f32[8,128]{1,0:T(8,128)}, u32[]{:S(2)}) copy-start(f32[8,128]{1,0:T(8,128)} %link_ref.1) | copy-start | bytes 12292
  3.2 12.8 %copy-start.11 = (f32[8,128]{1,0:T(8,128)S(1)}, f32[8,128]{1,0:T(8,128)}, u32[]{:S(2)}) copy-start(f32[8,128]{1,0:T(8,128)} %heel_ref.1) | copy-start | bytes 12292
  3.2 29.2 %all-to-all-start = ((f32[32,1,3200]{2,1,0:T(1,128)}), f32[32,1,3200]{2,1,0:T(1,128)S(1)}, u32[]{:S(2)}, u32[]{:S(2)}) async-start(f32[32,1,3200]{2,1,0:T(1,128)} %bitcast.3), calls=%async_computation | async-start | bytes 819200 | tf_op jit(solution)/shard_map/all_to_all | solution.py:408
  16.1 12.6 %copy-start.5 = (f32[3,8,8,128]{3,2,1,0:T(8,128)S(1)}, f32[3,8,8,128]{3,2,1,0:T(8,128)}, u32[]{:S(2)}) copy-start(f32[3,8,8,128]{3,2,1,0:T(8,128)} %param.18) | copy-start | bytes 294916
  16.1 12.6 %copy-start.7 = (f32[8,8,128]{2,1,0:T(8,128)S(1)}, f32[8,8,128]{2,1,0:T(8,128)}, u32[]{:S(2)}) copy-start(f32[8,8,128]{2,1,0:T(8,128)} %param.19) | copy-start | bytes 98308
  16.4 12.3 %collective-permute-start.1 = (f32[96,128]{1,0:T(8,128)S(1)}, f32[96,128]{1,0:T(8,128)S(1)}, u32[]{:S(2)}, u32[]{:S(2)}) collective-permute-start(f32[96,128]{1,0:T(8,128)S(1)} %get-tuple-element.20.xhi_ref), channel_id=1, source_target_pairs={{0,16},{16,32},{32,48},{48,64},{64,80},{80,96},{96,112},{112,128},... | collective-permute-start | bytes 147464 | tf_op jit(solution)/shard_map/ppermute | solution.py:387
  19.7 8.9 %collective-permute-start = (f32[80,128]{1,0:T(8,128)S(1)}, f32[80,128]{1,0:T(8,128)S(1)}, u32[]{:S(2)}, u32[]{:S(2)}) collective-permute-start(f32[80,128]{1,0:T(8,128)S(1)} %get-tuple-element.19.xlo_ref), channel_id=1, source_target_pairs={{16,0},{32,16},{48,32},{64,48},{80,64},{96,80},{112,96},{128,112},... | collective-permute-start | bytes 122888 | tf_op jit(solution)/shard_map/ppermute | solution.py:387
  24.3 5.1 %collective-permute-start.2 = (f32[8,128]{1,0:T(8,128)S(1)}, f32[8,128]{1,0:T(8,128)S(1)}, u32[]{:S(2)}, u32[]{:S(2)}) collective-permute-start(f32[8,128]{1,0:T(8,128)S(1)} %get-tuple-element.26.ylo_ref), channel_id=1, source_target_pairs={{1,0},{2,1},{3,2},{4,3},{5,4},{6,5},{7,6},{8,7},{9,8},{10,9},{11,1... | collective-permute-start | bytes 12296 | tf_op jit(solution)/shard_map/ppermute | solution.py:387
  26.3 6.1 %collective-permute-start.3 = (f32[8,128]{1,0:T(8,128)S(1)}, f32[8,128]{1,0:T(8,128)S(1)}, u32[]{:S(2)}, u32[]{:S(2)}) collective-permute-start(f32[8,128]{1,0:T(8,128)S(1)} %get-tuple-element.27.yhi_ref), channel_id=1, source_target_pairs={{0,1},{1,2},{2,3},{3,4},{4,5},{5,6},{6,7},{7,8},{8,9},{9,10},{10,1... | collective-permute-start | bytes 12296 | tf_op jit(solution)/shard_map/ppermute | solution.py:387

commit v5 on v4

--- a/solution.py
+++ b/solution.py
@@ -276,19 +276,20 @@
     edge = jnp.logical_or(lane == 0, lane == LANES - 1)
 
     seg_row = slot_ref[13:14, :].astype(jnp.int32) >> 7
+    own_tile = iota((8, LANES), 0) == group
     rates = [[] for _ in range(9)]
     for w in range(4):
         cols = slice(w * LANES, (w + 1) * LANES)
-        blocks = [got_ref[pl.ds(PLACE[w * 8 + k] * BLOCK, ROWS_A), :] for k in range(8)]
+        start = PLACE[w * 8] * BLOCK
+        blocks = [got_ref[pl.ds(start + r, 8, stride=2 * BLOCK), :] for r in range(ROWS_A)]
         hi, lo = split(jnp.concatenate(blocks, 0))
         picked = jnp.dot(jnp.concatenate([hi, lo], 1), seg_hot_ref[w], preferred_element_type=F32)
-        mine = picked[0:ROWS_A]
-        for k in range(1, 8):
-            mine = jnp.where(group == k, picked[k * ROWS_A:(k + 1) * ROWS_A], mine)
-        row_mask = iota((8, LANES), 0) == seg_row[:, cols]
-        at_seg = [
-            jnp.sum(jnp.where(row_mask, mine[s * 8:(s + 1) * 8], 0.0), axis=0, keepdims=True) for s in range(3)
-        ]
+        at_seg = []
+        for s in range(3):
+            mine = picked[s * 64:s * 64 + 8]
+            for r in range(1, 8):
+                mine = jnp.where(seg_row[:, cols] == r, picked[s * 64 + r * 8:s * 64 + r * 8 + 8], mine)
+            at_seg.append(jnp.sum(jnp.where(own_tile, mine, 0.0), axis=0, keepdims=True))
         drop = [slot_ref[s:s + 1, cols] - at_seg[s] for s in range(3)]
         base = [slot_ref[3 + a:4 + a, cols] for a in range(3)]
         for a in range(3):

time: 34.1 us -> 34.1 us (level)
  no operation moved by 1% of the time
where the time goes in v5:
time: 34.1 us; the launch traced here: 33.7 us
  starting transfers between devices  25 us (73%)
  Pallas kernels  4.82 us (14%)
  waiting for transfers between devices  2.94 us (9%)
  between operations  0.9 us (3%)
    all_to_all x1, starting transfers between devices, body(): lax.all_to_all(pay.reshape(TILES, 1, BLOCK * LANES), 'xt', 0, 0, tiled=Tr...  12.7 us
    ppermute x4, starting transfers between devices, shift(): lax.ppermute(array, axis, [(i, i + by) for i in range(length) if 0 <= i +...  12.3 us
    pallas_call x4, Pallas kernels, call(): pl.pallas_call(kernel, out_shape=[jax.ShapeDtypeStruct(o, F32) if isinsta...  4.82 us
    ppermute x4, waiting for transfers between devices, shift(): lax.ppermute(array, axis, [(i, i + by) for i in range(length) if 0 <= i +...  2.94 us
  transfers between devices with their start and end apart: 5, of which 1 were waited for; matrix products, arithmetic and copies ran while one was open for 0% of the time, Pallas kernels for 3%

profile of v5, /device:TPU:96, one launch (start us, length us, event | category | flops | bytes accessed | tf_op | source)
XLA Modules:
  0.0 33.7 jit_solution(11427517415584910617)
XLA Ops:
  0.6 2.5 %shard_map.175 = (f32[800,128]{1,0:T(8,128)}, f32[16,512]{1,0:T(8,128)S(1)}) custom-call(f32[64,128]{1,0:T(8,128)} %bitcast.20, f32[2,64,128]{2,1,0:T(8,128)} %bitcast.15, f32[2,3,64,128]{3,2,1,0:T(8,128)} %bitcast.11, f32[8,128]{1,0:T(8,128)} %sp_ref.1, f32[2,8,128]{2,1,0:T(8,128)} %st_ref.1, s32[1,512]{1,0:T(1,128)} %pc_hbm.1, s32[1,512]{1,0:T(1,128)} %ps_hbm.1, ...), custom_call_target="tpu_custom_call" | custom-call | tf_op jit(solution)/shard_map/pallas_call | solution.py:370
  3.1 0.0 copy-start
  3.1 0.0 copy-start.1
  3.1 0.0 copy-start.2
  3.2 0.0 copy-start.3
  3.2 0.0 copy-start.4
  3.2 0.0 copy-start.6
  3.2 0.0 copy-start.8
  3.2 0.0 copy-start.9
  3.2 0.0 copy-start.10
  3.2 0.0 copy-start.11
  3.2 12.7 %all-to-all-start = ((f32[32,1,3200]{2,1,0:T(1,128)}), f32[32,1,3200]{2,1,0:T(1,128)S(1)}, u32[]{:S(2)}, u32[]{:S(2)}) async-start(f32[32,1,3200]{2,1,0:T(1,128)} %bitcast.3), calls=%async_computation | async-start | bytes 819200 | tf_op jit(solution)/shard_map/all_to_all | solution.py:409
  16.0 0.0 copy-done
  16.0 0.0 copy-done.1
  16.0 0.0 copy-done.2
  16.0 0.0 copy-done.3
  16.0 0.0 copy-done.4
  16.0 0.0 copy-done.6
  16.0 0.0 copy-done.8
  16.1 0.0 copy-done.9
  16.1 0.0 copy-done.10
  16.1 0.0 copy-done.11
  16.1 0.0 copy-start.5
  16.1 0.0 copy-start.7
  16.1 0.2 shard_map.176
  16.4 3.4 %collective-permute-start.1 = (f32[96,128]{1,0:T(8,128)S(1)}, f32[96,128]{1,0:T(8,128)S(1)}, u32[]{:S(2)}, u32[]{:S(2)}) collective-permute-start(f32[96,128]{1,0:T(8,128)S(1)} %get-tuple-element.20.xhi_ref), channel_id=1, source_target_pairs={{0,16},{16,32},{32,48},{48,64},{64,80},{80,96},{96,112},{112,128},... | collective-permute-start | bytes 147464 | tf_op jit(solution)/shard_map/ppermute | solution.py:388
  19.7 4.6 %collective-permute-start = (f32[80,128]{1,0:T(8,128)S(1)}, f32[80,128]{1,0:T(8,128)S(1)}, u32[]{:S(2)}, u32[]{:S(2)}) collective-permute-start(f32[80,128]{1,0:T(8,128)S(1)} %get-tuple-element.19.xlo_ref), channel_id=1, source_target_pairs={{16,0},{32,16},{48,32},{64,48},{80,64},{96,80},{112,96},{128,112},... | collective-permute-start | bytes 122888 | tf_op jit(solution)/shard_map/ppermute | solution.py:388
  24.3 1.9 %collective-permute-start.2 = (f32[8,128]{1,0:T(8,128)S(1)}, f32[8,128]{1,0:T(8,128)S(1)}, u32[]{:S(2)}, u32[]{:S(2)}) collective-permute-start(f32[8,128]{1,0:T(8,128)S(1)} %get-tuple-element.26.ylo_ref), channel_id=1, source_target_pairs={{1,0},{2,1},{3,2},{4,3},{5,4},{6,5},{7,6},{8,7},{9,8},{10,9},{11,1... | collective-permute-start | bytes 12296 | tf_op jit(solution)/shard_map/ppermute | solution.py:388
  26.3 2.4 %collective-permute-start.3 = (f32[8,128]{1,0:T(8,128)S(1)}, f32[8,128]{1,0:T(8,128)S(1)}, u32[]{:S(2)}, u32[]{:S(2)}) collective-permute-start(f32[8,128]{1,0:T(8,128)S(1)} %get-tuple-element.27.yhi_ref), channel_id=1, source_target_pairs={{0,1},{1,2},{2,3},{3,4},{4,5},{5,6},{6,7},{7,8},{8,9},{9,10},{10,1... | collective-permute-start | bytes 12296 | tf_op jit(solution)/shard_map/ppermute | solution.py:388
  28.7 0.0 collective-permute-done.exlo_ref
  28.7 0.0 collective-permute-done.1.wxhi_ref
  28.7 0.0 copy-done.5
  28.7 0.0 copy-done.7
  28.7 0.7 %shard_map.177 = (f32[9,64,128]{2,1,0:T(8,128)S(1)}, bf16[1024,256]{1,0:T(8,128)(2,1)S(1)}, bf16[32,512]{1,0:T(8,128)(2,1)S(1)}, bf16[4,256,128]{2,1,0:T(8,128)(2,1)S(1)}) custom-call(f32[64,128]{1,0:T(8,128)S(1)} %bitcast.22, f32[2,64,128]{2,1,0:T(8,128)S(1)} %bitcast.17, f32[2,3,64,128]{3,2,1,0:T(8,128)S(1)} %bitcast.13, f32[3,64,128]{2,1,0:T(8,128)S(1)} %bitcast.25, ...), custom_call_target="tpu_custom_call" | custom-call | tf_op jit(solution)/shard_map/pallas_call | solution.py:370
  29.5 0.0 collective-permute-done.2.nylo_ref
  29.5 2.9 %collective-permute-done.3.syhi_ref = f32[8,128]{1,0:T(8,128)S(1)} collective-permute-done((f32[8,128]{1,0:T(8,128)S(1)}, f32[8,128]{1,0:T(8,128)S(1)}, u32[]{:S(2)}, u32[]{:S(2)}) %collective-permute-start.3) | collective-permute-done | bytes 4128 | tf_op jit(solution)/shard_map/ppermute | solution.py:388
  32.4 0.0 all-to-all-done
  32.4 1.4 %shard_map.178 = (f32[3,64,128]{2,1,0:T(8,128)}, f32[2,3,64,128]{3,2,1,0:T(8,128)}, f32[3,8,128]{2,1,0:T(8,128)}) custom-call(f32[800,128]{1,0:T(8,128)S(1)} %bitcast.14, f32[16,512]{1,0:T(8,128)S(1)} %get-tuple-element.18.slot_ref, f32[9,64,128]{2,1,0:T(8,128)S(1)} %get-tuple-element.21.bal_ref, f32[48,128]{1,0:T(8,128)S(1)} %get-tuple-element.22.seg_ref, ...), custom_call_target="tpu_custom_call" | custom-call | tf_op jit(solution)/shard_map/pallas_call | solution.py:370
Async XLA Ops:
  3.1 12.9 %copy-start = (f32[2,3,8,8,128]{4,3,2,1,0:T(8,128)S(1)}, f32[2,3,8,8,128]{4,3,2,1,0:T(8,128)}, u32[]{:S(2)}) copy-start(f32[2,3,8,8,128]{4,3,2,1,0:T(8,128)} %param.22) | copy-start | bytes 589828
  3.1 12.9 %copy-start.1 = (f32[2,8,8,128]{3,2,1,0:T(8,128)S(1)}, f32[2,8,8,128]{3,2,1,0:T(8,128)}, u32[]{:S(2)}) copy-start(f32[2,8,8,128]{3,2,1,0:T(8,128)} %param.17) | copy-start | bytes 196612
  3.1 12.9 %copy-start.2 = (f32[3,8,8,128]{3,2,1,0:T(8,128)S(1)}, f32[3,8,8,128]{3,2,1,0:T(8,128)}, u32[]{:S(2)}) copy-start(f32[3,8,8,128]{3,2,1,0:T(8,128)} %param.20) | copy-start | bytes 294916
  3.2 12.9 %copy-start.3 = (f32[8,8,128]{2,1,0:T(8,128)S(1)}, f32[8,8,128]{2,1,0:T(8,128)}, u32[]{:S(2)}) copy-start(f32[8,8,128]{2,1,0:T(8,128)} %param.16) | copy-start | bytes 98308
  3.2 12.9 %copy-start.4 = (s32[8,8,128]{2,1,0:T(8,128)S(1)}, s32[8,8,128]{2,1,0:T(8,128)}, u32[]{:S(2)}) copy-start(s32[8,8,128]{2,1,0:T(8,128)} %param.21) | copy-start | bytes 98308
  3.2 12.8 %copy-start.6 = (f32[2,8,128]{2,1,0:T(8,128)S(1)}, f32[2,8,128]{2,1,0:T(8,128)}, u32[]{:S(2)}) copy-start(f32[2,8,128]{2,1,0:T(8,128)} %st_ref.1) | copy-start | bytes 24580
  3.2 12.8 %copy-start.8 = (f32[8,128]{1,0:T(8,128)S(1)}, f32[8,128]{1,0:T(8,128)}, u32[]{:S(2)}) copy-start(f32[8,128]{1,0:T(8,128)} %sp_ref.1) | copy-start | bytes 12292
  3.2 12.8 %copy-start.9 = (s32[8,128]{1,0:T(8,128)S(1)}, s32[8,128]{1,0:T(8,128)}, u32[]{:S(2)}) copy-start(s32[8,128]{1,0:T(8,128)} %well_ref.1) | copy-start | bytes 12292
  3.2 12.8 %copy-start.10 = (f32[8,128]{1,0:T(8,128)S(1)}, f32[8,128]{1,0:T(8,128)}, u32[]{:S(2)}) copy-start(f32[8,128]{1,0:T(8,128)} %link_ref.1) | copy-start | bytes 12292
  3.2 12.8 %copy-start.11 = (f32[8,128]{1,0:T(8,128)S(1)}, f32[8,128]{1,0:T(8,128)}, u32[]{:S(2)}) copy-start(f32[8,128]{1,0:T(8,128)} %heel_ref.1) | copy-start | bytes 12292
  3.2 29.2 %all-to-all-start = ((f32[32,1,3200]{2,1,0:T(1,128)}), f32[32,1,3200]{2,1,0:T(1,128)S(1)}, u32[]{:S(2)}, u32[]{:S(2)}) async-start(f32[32,1,3200]{2,1,0:T(1,128)} %bitcast.3), calls=%async_computation | async-start | bytes 819200 | tf_op jit(solution)/shard_map/all_to_all | solution.py:409
  16.1 12.6 %copy-start.5 = (f32[3,8,8,128]{3,2,1,0:T(8,128)S(1)}, f32[3,8,8,128]{3,2,1,0:T(8,128)}, u32[]{:S(2)}) copy-start(f32[3,8,8,128]{3,2,1,0:T(8,128)} %param.18) | copy-start | bytes 294916
  16.1 12.6 %copy-start.7 = (f32[8,8,128]{2,1,0:T(8,128)S(1)}, f32[8,8,128]{2,1,0:T(8,128)}, u32[]{:S(2)}) copy-start(f32[8,8,128]{2,1,0:T(8,128)} %param.19) | copy-start | bytes 98308
  16.4 12.3 %collective-permute-start.1 = (f32[96,128]{1,0:T(8,128)S(1)}, f32[96,128]{1,0:T(8,128)S(1)}, u32[]{:S(2)}, u32[]{:S(2)}) collective-permute-start(f32[96,128]{1,0:T(8,128)S(1)} %get-tuple-element.20.xhi_ref), channel_id=1, source_target_pairs={{0,16},{16,32},{32,48},{48,64},{64,80},{80,96},{96,112},{112,128},... | collective-permute-start | bytes 147464 | tf_op jit(solution)/shard_map/ppermute | solution.py:388
  19.7 8.9 %collective-permute-start = (f32[80,128]{1,0:T(8,128)S(1)}, f32[80,128]{1,0:T(8,128)S(1)}, u32[]{:S(2)}, u32[]{:S(2)}) collective-permute-start(f32[80,128]{1,0:T(8,128)S(1)} %get-tuple-element.19.xlo_ref), channel_id=1, source_target_pairs={{16,0},{32,16},{48,32},{64,48},{80,64},{96,80},{112,96},{128,112},... | collective-permute-start | bytes 122888 | tf_op jit(solution)/shard_map/ppermute | solution.py:388
  24.3 5.1 %collective-permute-start.2 = (f32[8,128]{1,0:T(8,128)S(1)}, f32[8,128]{1,0:T(8,128)S(1)}, u32[]{:S(2)}, u32[]{:S(2)}) collective-permute-start(f32[8,128]{1,0:T(8,128)S(1)} %get-tuple-element.26.ylo_ref), channel_id=1, source_target_pairs={{1,0},{2,1},{3,2},{4,3},{5,4},{6,5},{7,6},{8,7},{9,8},{10,9},{11,1... | collective-permute-start | bytes 12296 | tf_op jit(solution)/shard_map/ppermute | solution.py:388
  26.3 6.1 %collective-permute-start.3 = (f32[8,128]{1,0:T(8,128)S(1)}, f32[8,128]{1,0:T(8,128)S(1)}, u32[]{:S(2)}, u32[]{:S(2)}) collective-permute-start(f32[8,128]{1,0:T(8,128)S(1)} %get-tuple-element.27.yhi_ref), channel_id=1, source_target_pairs={{0,1},{1,2},{2,3},{3,4},{4,5},{5,6},{6,7},{7,8},{8,9},{9,10},{10,1... | collective-permute-start | bytes 12296 | tf_op jit(solution)/shard_map/ppermute | solution.py:388

commit v6 on v5

--- a/solution.py
+++ b/solution.py
@@ -115,9 +115,9 @@
     tile_hot = one_hot(iota((TILES, SLOTS), 0) == owner)
     copies[0].wait()
     cell = pc_ref[...]
-    lane_hot = one_hot(iota((LANES, SLOTS), 0) == (cell & (LANES - 1)))
+    lane_hot = one_hot(iota((WIDE, SLOTS), 0) == (cell & (WIDE - 1)))
     lane_hot = jnp.concatenate([lane_hot, lane_hot], 0)
-    row_mask = iota((CELL_ROWS, SLOTS), 0) == (cell >> 7)
+    row_mask = iota((WIDE_ROWS, SLOTS), 0) == (cell >> 8)
     for copy in copies[1:6]:
         copy.wait()
     seg = [sp_ref[...], st_ref[0], st_ref[1]]
@@ -131,11 +131,11 @@
     number = ps_ref[...].astype(F32)
     for copy in copies[6:]:
         copy.wait()
-    at = pl.ds(0, CELL_ROWS)
-    hi, lo = split(jnp.concatenate(nine(p_ref, s_ref, ct_ref, at), 0))
+    halves = [nine(p_ref, s_ref, ct_ref, pl.ds(h, WIDE_ROWS, stride=2)) for h in range(2)]
+    hi, lo = split(jnp.concatenate([jnp.concatenate(half, 0) for half in halves], 1))
     picked = jnp.dot(jnp.concatenate([hi, lo], 1), lane_hot, preferred_element_type=F32)
     val = [
-        jnp.sum(jnp.where(row_mask, picked[q * CELL_ROWS:(q + 1) * CELL_ROWS], 0.0), axis=0, keepdims=True)
+        jnp.sum(jnp.where(row_mask, picked[q * WIDE_ROWS:(q + 1) * WIDE_ROWS], 0.0), axis=0, keepdims=True)
         for q in range(9)
     ]
     press = val[0:3]

time: 34.1 us -> 34.1 us (level)
  no operation moved by 1% of the time
where the time goes in v6:
time: 34.1 us; the launch traced here: 33.8 us
  starting transfers between devices  25 us (73%)
  Pallas kernels  4.83 us (14%)
  waiting for transfers between devices  2.94 us (9%)
  between operations  0.9 us (3%)
    all_to_all x1, starting transfers between devices, body(): lax.all_to_all(pay.reshape(TILES, 1, BLOCK * LANES), 'xt', 0, 0, tiled=Tr...  12.7 us
    ppermute x4, starting transfers between devices, shift(): lax.ppermute(array, axis, [(i, i + by) for i in range(length) if 0 <= i +...  12.3 us
    pallas_call x4, Pallas kernels, call(): pl.pallas_call(kernel, out_shape=[jax.ShapeDtypeStruct(o, F32) if isinsta...  4.83 us
    ppermute x4, waiting for transfers between devices, shift(): lax.ppermute(array, axis, [(i, i + by) for i in range(length) if 0 <= i +...  2.94 us
  transfers between devices with their start and end apart: 5, of which 1 were waited for; matrix products, arithmetic and copies ran while one was open for 0% of the time, Pallas kernels for 3%

profile of v6, /device:TPU:96, one launch (start us, length us, event | category | flops | bytes accessed | tf_op | source)
XLA Modules:
  0.0 33.8 jit_solution(17594461429579175320)
XLA Ops:
  0.6 2.5 %shard_map.175 = (f32[800,128]{1,0:T(8,128)}, f32[16,512]{1,0:T(8,128)S(1)}) custom-call(f32[64,128]{1,0:T(8,128)} %bitcast.20, f32[2,64,128]{2,1,0:T(8,128)} %bitcast.15, f32[2,3,64,128]{3,2,1,0:T(8,128)} %bitcast.11, f32[8,128]{1,0:T(8,128)} %sp_ref.1, f32[2,8,128]{2,1,0:T(8,128)} %st_ref.1, s32[1,512]{1,0:T(1,128)} %pc_hbm.1, s32[1,512]{1,0:T(1,128)} %ps_hbm.1, ...), custom_call_target="tpu_custom_call" | custom-call | tf_op jit(solution)/shard_map/pallas_call | solution.py:370
  3.1 0.0 copy-start
  3.1 0.0 copy-start.1
  3.2 0.0 copy-start.2
  3.2 0.0 copy-start.3
  3.2 0.0 copy-start.4
  3.2 0.0 copy-start.6
  3.2 0.0 copy-start.8
  3.2 0.0 copy-start.9
  3.2 0.0 copy-start.10
  3.2 0.0 copy-start.11
  3.3 12.7 %all-to-all-start = ((f32[32,1,3200]{2,1,0:T(1,128)}), f32[32,1,3200]{2,1,0:T(1,128)S(1)}, u32[]{:S(2)}, u32[]{:S(2)}) async-start(f32[32,1,3200]{2,1,0:T(1,128)} %bitcast.3), calls=%async_computation | async-start | bytes 819200 | tf_op jit(solution)/shard_map/all_to_all | solution.py:409
  16.0 0.0 copy-done
  16.0 0.0 copy-done.1
  16.0 0.0 copy-done.2
  16.0 0.0 copy-done.3
  16.0 0.0 copy-done.4
  16.0 0.0 copy-done.6
  16.0 0.0 copy-done.8
  16.1 0.0 copy-done.9
  16.1 0.0 copy-done.10
  16.1 0.0 copy-done.11
  16.1 0.0 copy-start.5
  16.1 0.0 copy-start.7
  16.1 0.2 shard_map.176
  16.4 3.4 %collective-permute-start.1 = (f32[96,128]{1,0:T(8,128)S(1)}, f32[96,128]{1,0:T(8,128)S(1)}, u32[]{:S(2)}, u32[]{:S(2)}) collective-permute-start(f32[96,128]{1,0:T(8,128)S(1)} %get-tuple-element.20.xhi_ref), channel_id=1, source_target_pairs={{0,16},{16,32},{32,48},{48,64},{64,80},{80,96},{96,112},{112,128},... | collective-permute-start | bytes 147464 | tf_op jit(solution)/shard_map/ppermute | solution.py:388
  19.7 4.6 %collective-permute-start = (f32[80,128]{1,0:T(8,128)S(1)}, f32[80,128]{1,0:T(8,128)S(1)}, u32[]{:S(2)}, u32[]{:S(2)}) collective-permute-start(f32[80,128]{1,0:T(8,128)S(1)} %get-tuple-element.19.xlo_ref), channel_id=1, source_target_pairs={{16,0},{32,16},{48,32},{64,48},{80,64},{96,80},{112,96},{128,112},... | collective-permute-start | bytes 122888 | tf_op jit(solution)/shard_map/ppermute | solution.py:388
  24.3 1.9 %collective-permute-start.2 = (f32[8,128]{1,0:T(8,128)S(1)}, f32[8,128]{1,0:T(8,128)S(1)}, u32[]{:S(2)}, u32[]{:S(2)}) collective-permute-start(f32[8,128]{1,0:T(8,128)S(1)} %get-tuple-element.26.ylo_ref), channel_id=1, source_target_pairs={{1,0},{2,1},{3,2},{4,3},{5,4},{6,5},{7,6},{8,7},{9,8},{10,9},{11,1... | collective-permute-start | bytes 12296 | tf_op jit(solution)/shard_map/ppermute | solution.py:388
  26.3 2.4 %collective-permute-start.3 = (f32[8,128]{1,0:T(8,128)S(1)}, f32[8,128]{1,0:T(8,128)S(1)}, u32[]{:S(2)}, u32[]{:S(2)}) collective-permute-start(f32[8,128]{1,0:T(8,128)S(1)} %get-tuple-element.27.yhi_ref), channel_id=1, source_target_pairs={{0,1},{1,2},{2,3},{3,4},{4,5},{5,6},{6,7},{7,8},{8,9},{9,10},{10,1... | collective-permute-start | bytes 12296 | tf_op jit(solution)/shard_map/ppermute | solution.py:388
  28.7 0.0 collective-permute-done.exlo_ref
  28.7 0.0 collective-permute-done.1.wxhi_ref
  28.7 0.0 copy-done.5
  28.7 0.0 copy-done.7
  28.7 0.7 %shard_map.177 = (f32[9,64,128]{2,1,0:T(8,128)S(1)}, bf16[1024,256]{1,0:T(8,128)(2,1)S(1)}, bf16[32,512]{1,0:T(8,128)(2,1)S(1)}, bf16[4,256,128]{2,1,0:T(8,128)(2,1)S(1)}) custom-call(f32[64,128]{1,0:T(8,128)S(1)} %bitcast.22, f32[2,64,128]{2,1,0:T(8,128)S(1)} %bitcast.17, f32[2,3,64,128]{3,2,1,0:T(8,128)S(1)} %bitcast.13, f32[3,64,128]{2,1,0:T(8,128)S(1)} %bitcast.25, ...), custom_call_target="tpu_custom_call" | custom-call | tf_op jit(solution)/shard_map/pallas_call | solution.py:370
  29.5 0.0 collective-permute-done.2.nylo_ref
  29.5 2.9 %collective-permute-done.3.syhi_ref = f32[8,128]{1,0:T(8,128)S(1)} collective-permute-done((f32[8,128]{1,0:T(8,128)S(1)}, f32[8,128]{1,0:T(8,128)S(1)}, u32[]{:S(2)}, u32[]{:S(2)}) %collective-permute-start.3) | collective-permute-done | bytes 4128 | tf_op jit(solution)/shard_map/ppermute | solution.py:388
  32.4 0.0 all-to-all-done
  32.4 1.4 %shard_map.178 = (f32[3,64,128]{2,1,0:T(8,128)}, f32[2,3,64,128]{3,2,1,0:T(8,128)}, f32[3,8,128]{2,1,0:T(8,128)}) custom-call(f32[800,128]{1,0:T(8,128)S(1)} %bitcast.14, f32[16,512]{1,0:T(8,128)S(1)} %get-tuple-element.18.slot_ref, f32[9,64,128]{2,1,0:T(8,128)S(1)} %get-tuple-element.21.bal_ref, f32[48,128]{1,0:T(8,128)S(1)} %get-tuple-element.22.seg_ref, ...), custom_call_target="tpu_custom_call" | custom-call | tf_op jit(solution)/shard_map/pallas_call | solution.py:370
Async XLA Ops:
  3.1 12.9 %copy-start = (f32[2,3,8,8,128]{4,3,2,1,0:T(8,128)S(1)}, f32[2,3,8,8,128]{4,3,2,1,0:T(8,128)}, u32[]{:S(2)}) copy-start(f32[2,3,8,8,128]{4,3,2,1,0:T(8,128)} %param.22) | copy-start | bytes 589828
  3.1 12.9 %copy-start.1 = (f32[2,8,8,128]{3,2,1,0:T(8,128)S(1)}, f32[2,8,8,128]{3,2,1,0:T(8,128)}, u32[]{:S(2)}) copy-start(f32[2,8,8,128]{3,2,1,0:T(8,128)} %param.17) | copy-start | bytes 196612
  3.2 12.9 %copy-start.2 = (f32[3,8,8,128]{3,2,1,0:T(8,128)S(1)}, f32[3,8,8,128]{3,2,1,0:T(8,128)}, u32[]{:S(2)}) copy-start(f32[3,8,8,128]{3,2,1,0:T(8,128)} %param.20) | copy-start | bytes 294916
  3.2 12.9 %copy-start.3 = (f32[8,8,128]{2,1,0:T(8,128)S(1)}, f32[8,8,128]{2,1,0:T(8,128)}, u32[]{:S(2)}) copy-start(f32[8,8,128]{2,1,0:T(8,128)} %param.16) | copy-start | bytes 98308
  3.2 12.9 %copy-start.4 = (s32[8,8,128]{2,1,0:T(8,128)S(1)}, s32[8,8,128]{2,1,0:T(8,128)}, u32[]{:S(2)}) copy-start(s32[8,8,128]{2,1,0:T(8,128)} %param.21) | copy-start | bytes 98308
  3.2 12.8 %copy-start.6 = (f32[2,8,128]{2,1,0:T(8,128)S(1)}, f32[2,8,128]{2,1,0:T(8,128)}, u32[]{:S(2)}) copy-start(f32[2,8,128]{2,1,0:T(8,128)} %st_ref.1) | copy-start | bytes 24580
  3.2 12.8 %copy-start.8 = (f32[8,128]{1,0:T(8,128)S(1)}, f32[8,128]{1,0:T(8,128)}, u32[]{:S(2)}) copy-start(f32[8,128]{1,0:T(8,128)} %sp_ref.1) | copy-start | bytes 12292
  3.2 12.8 %copy-start.9 = (s32[8,128]{1,0:T(8,128)S(1)}, s32[8,128]{1,0:T(8,128)}, u32[]{:S(2)}) copy-start(s32[8,128]{1,0:T(8,128)} %well_ref.1) | copy-start | bytes 12292
  3.2 12.8 %copy-start.10 = (f32[8,128]{1,0:T(8,128)S(1)}, f32[8,128]{1,0:T(8,128)}, u32[]{:S(2)}) copy-start(f32[8,128]{1,0:T(8,128)} %link_ref.1) | copy-start | bytes 12292
  3.2 12.8 %copy-start.11 = (f32[8,128]{1,0:T(8,128)S(1)}, f32[8,128]{1,0:T(8,128)}, u32[]{:S(2)}) copy-start(f32[8,128]{1,0:T(8,128)} %heel_ref.1) | copy-start | bytes 12292
  3.3 29.2 %all-to-all-start = ((f32[32,1,3200]{2,1,0:T(1,128)}), f32[32,1,3200]{2,1,0:T(1,128)S(1)}, u32[]{:S(2)}, u32[]{:S(2)}) async-start(f32[32,1,3200]{2,1,0:T(1,128)} %bitcast.3), calls=%async_computation | async-start | bytes 819200 | tf_op jit(solution)/shard_map/all_to_all | solution.py:409
  16.1 12.6 %copy-start.5 = (f32[3,8,8,128]{3,2,1,0:T(8,128)S(1)}, f32[3,8,8,128]{3,2,1,0:T(8,128)}, u32[]{:S(2)}) copy-start(f32[3,8,8,128]{3,2,1,0:T(8,128)} %param.18) | copy-start | bytes 294916
  16.1 12.6 %copy-start.7 = (f32[8,8,128]{2,1,0:T(8,128)S(1)}, f32[8,8,128]{2,1,0:T(8,128)}, u32[]{:S(2)}) copy-start(f32[8,8,128]{2,1,0:T(8,128)} %param.19) | copy-start | bytes 98308
  16.4 12.3 %collective-permute-start.1 = (f32[96,128]{1,0:T(8,128)S(1)}, f32[96,128]{1,0:T(8,128)S(1)}, u32[]{:S(2)}, u32[]{:S(2)}) collective-permute-start(f32[96,128]{1,0:T(8,128)S(1)} %get-tuple-element.20.xhi_ref), channel_id=1, source_target_pairs={{0,16},{16,32},{32,48},{48,64},{64,80},{80,96},{96,112},{112,128},... | collective-permute-start | bytes 147464 | tf_op jit(solution)/shard_map/ppermute | solution.py:388
  19.7 8.9 %collective-permute-start = (f32[80,128]{1,0:T(8,128)S(1)}, f32[80,128]{1,0:T(8,128)S(1)}, u32[]{:S(2)}, u32[]{:S(2)}) collective-permute-start(f32[80,128]{1,0:T(8,128)S(1)} %get-tuple-element.19.xlo_ref), channel_id=1, source_target_pairs={{16,0},{32,16},{48,32},{64,48},{80,64},{96,80},{112,96},{128,112},... | collective-permute-start | bytes 122888 | tf_op jit(solution)/shard_map/ppermute | solution.py:388
  24.3 5.1 %collective-permute-start.2 = (f32[8,128]{1,0:T(8,128)S(1)}, f32[8,128]{1,0:T(8,128)S(1)}, u32[]{:S(2)}, u32[]{:S(2)}) collective-permute-start(f32[8,128]{1,0:T(8,128)S(1)} %get-tuple-element.26.ylo_ref), channel_id=1, source_target_pairs={{1,0},{2,1},{3,2},{4,3},{5,4},{6,5},{7,6},{8,7},{9,8},{10,9},{11,1... | collective-permute-start | bytes 12296 | tf_op jit(solution)/shard_map/ppermute | solution.py:388
  26.3 6.1 %collective-permute-start.3 = (f32[8,128]{1,0:T(8,128)S(1)}, f32[8,128]{1,0:T(8,128)S(1)}, u32[]{:S(2)}, u32[]{:S(2)}) collective-permute-start(f32[8,128]{1,0:T(8,128)S(1)} %get-tuple-element.27.yhi_ref), channel_id=1, source_target_pairs={{0,1},{1,2},{2,3},{3,4},{4,5},{5,6},{6,7},{7,8},{8,9},{9,10},{10,1... | collective-permute-start | bytes 12296 | tf_op jit(solution)/shard_map/ppermute | solution.py:388
